TPU v7x, 128 devices: a whole 4x4x4 slice. The times are simulated.
128 devices in a mesh: morton: 128 (over y, z, x, core).
Axes of the slice: x: 4, y: 4, z: 4, core: 2. Of those that a mesh axis runs over, the one named last changes fastest.
Arguments:
- multipoles: bfloat16 [3, 488, 32768], P(None, None, 'morton'), may hold values from -6 to 6
- upward_ops: bfloat16 [8, 488, 488], replicated, may hold values from -0.25 to 0.25
- transfer_ops: bfloat16 [36, 488, 488], replicated, may hold values from -0.25 to 0.25
- live_counts: int32 [128], P('morton'), may hold values from 128 to 256, as said below
- seam_joins: int32 [128, 2], P('morton'), may hold values from 0 to 1, as said below
- send_slots: int32 [128, 1024], P('morton'), may hold values from 0 to 127
- vlist_cols: int32 [32768, 36], P('morton'), may hold values from 0 to 1280, as said below
Outputs:
- local_check: float32 [3, 488, 32768], P(None, None, 'morton')
- parent_mult: float32 [3, 488, 4096], P(None, None, 'morton')
Inputs may be any that keep to these rules, and one draw needn't show every extreme that they name: `live_counts`: some device has 256 boxes in use and some has 128. seam_joins[d, 0] equals seam_joins[d - 1, 1]; the first device's left entry and the last device's right entry are 0; the seam between the first two devices and the seam between the last two are always joined. `vlist_cols`: entries below 256 are the device's own slots, entries from 256 below 1280 are received ghost columns, and 1280 marks an absent source; every device uses every ghost column.
All inputs are finite; a program needn't handle non-finite values.
Results may differ from a plain program's by a relative error of at most 0.0003.
Values may be sent and summed in bfloat16 or wider, within the bound.
No kernel may reach another device: no remote copies, remote signals or barrier semaphores. Data moves between devices by JAX's collectives and lax.ppermute only.
A program may use at most 192 MiB of HBM per device.

v0:
```python
import jax
import jax.numpy as jnp
from jax import lax
from jax.sharding import PartitionSpec as P


def with_halo(cells, sides, width):
    for axis, dim in sides:
        count = lax.axis_size(axis)
        ends = count - 1
        head = lax.slice_in_dim(cells, 0, width, axis=dim)
        tail = lax.slice_in_dim(cells, cells.shape[dim] - width, cells.shape[dim], axis=dim)
        cells = jnp.concatenate(
            [
                lax.ppermute(tail, axis, [(i, (i + 1) % count) for i in range(ends)]),
                cells,
                lax.ppermute(head, axis, [((i + 1) % count, i) for i in range(ends)]),
            ],
            axis=dim,
        )
    return cells


def body(multipoles, upward_ops, transfer_ops, live_counts, seam_joins, send_slots, vlist_cols):
    channels, points, slot_total = multipoles.shape
    group_total = slot_total // 8
    dev_count = lax.axis_size("morton")
    ghost_total = send_slots.shape[1] // dev_count
    slot_ids = jnp.arange(slot_total, dtype=jnp.int32)
    keep = (slot_ids < live_counts[0])[None, None, :]
    masked = jnp.where(keep, multipoles, jnp.zeros_like(multipoles))
    children = masked.reshape(channels, points, group_total, 8)
    partial_value = jnp.einsum(
        "oij,cjgo->cig", upward_ops, children, preferred_element_type=jnp.float32
    )
    last_group = (live_counts[0] - 1) // 8
    last_part = lax.dynamic_slice_in_dim(partial_value, last_group, 1, 2)
    edge_rows = jnp.concatenate([partial_value[:, :, :1], last_part], axis=2)
    widened = with_halo(edge_rows, (("morton", 2),), 1)
    group_ids = jnp.arange(group_total, dtype=jnp.int32)
    join_left = seam_joins[0, 0].astype(jnp.float32)
    join_right = seam_joins[0, 1].astype(jnp.float32)
    parent_mult = partial_value + jnp.where(
        (group_ids == 0)[None, None, :],
        (join_left * widened[:, :, 0])[:, :, None],
        jnp.float32(0.0),
    )
    parent_mult = parent_mult + jnp.where(
        (group_ids == last_group)[None, None, :],
        (join_right * widened[:, :, 3])[:, :, None],
        jnp.float32(0.0),
    )
    box_rows = masked.reshape(channels * points, slot_total).T
    outgoing_rows = jnp.take(box_rows, send_slots[0], axis=0)
    outgoing = outgoing_rows.T.reshape(channels, points, dev_count * ghost_total)
    arrived = lax.all_to_all(outgoing, "morton", split_axis=2, concat_axis=2, tiled=True)
    arrived_rows = arrived.reshape(channels * points, dev_count * ghost_total).T
    zero_row = jnp.zeros((1, channels * points), multipoles.dtype)
    buffer_rows = jnp.concatenate([box_rows, arrived_rows, zero_row], axis=0)
    rel_count = vlist_cols.shape[1]
    picked_rows = jnp.take(buffer_rows, vlist_cols.T.reshape(-1), axis=0)
    picked_rows = picked_rows.reshape(rel_count, slot_total, channels, points)
    local_check = jnp.einsum(
        "rij,rbcj->cib", transfer_ops, picked_rows, preferred_element_type=jnp.float32
    )
    local_check = jnp.where(keep, local_check, jnp.float32(0.0))
    return (local_check, parent_mult)


def solution(mesh):
    placed = (
        P(None, None, "morton"),
        P(),
        P(),
        P("morton"),
        P("morton", None),
        P("morton", None),
        P("morton", None),
    )
    return jax.shard_map(
        body,
        mesh=mesh,
        in_specs=placed,
        out_specs=(P(None, None, "morton"), P(None, None, "morton")),
        check_vma=False,
    )
```

profile of v0, /device:TPU:1, one launch (start us, length us, event | category | flops | bytes accessed | tf_op | source)
XLA Modules:
  0.0 296.2 jit_solution(7956885168755238323)
XLA Ops:
  1.3 1.2 broadcast_select_fusion.1
  2.5 0.3 copy.26
  2.8 0.0 copy-start.1
  2.8 3.4 %fusion.3 = f32[3,32,488,1]{2,1,3,0:T(8,128)S(1)} fusion(bf16[8,488,488]{2,1,0:T(8,128)(2,1)} %param.8, bf16[3,488,32,8]{1,3,2,0:T(8,128)(2,1)S(1)} %bitcast.63), kind=kOutput, calls=%fused_computation.6 | convolution fusion | flops 365789184 | bytes 4747264 | tf_op jit(solution)/shard_map/oij,cjgo->cig/dot_general | solution.py:33
  6.2 4.5 %collective-permute-start = (f32[3,488,1]{1,2,0:T(1,128)S(1)}, f32[3,488,1]{1,2,0:T(1,128)S(1)}, u32[]{:S(2)}, u32[]{:S(2)}) collective-permute-start(f32[3,488,1]{1,2,0:T(1,128)S(1)} %dynamic-slice_bitcast_fusion), channel_id=1, source_target_pairs={{0,1},{1,2},{2,3},{3,4},{4,5},{5,6},{6,7},{7,8},{8,9},{9,10},{10,1... | collective-permute-start | bytes 17576 | tf_op jit(solution)/shard_map/ppermute | solution.py:15
  10.7 1.9 collective-permute-start.1
  12.7 0.3 copy.19
  12.9 0.0 copy-done.1
  13.0 5.6 %gather_fusion = bf16[1024,1464]{1,0:T(8,128)(2,1)} fusion(bf16[256,1464]{1,0:T(8,128)(2,1)S(1)} %bitcast.57, s32[1024]{0:T(1024)S(1)} %broadcast_clamp_fusion.1), kind=kCustom, calls=%fused_computation | custom fusion | bytes 6000640 | tf_op jit(solution)/shard_map/jit(_take)/gather | solution.py:54
  18.6 3.9 %select_bitcast_fusion = bf16[1464,1024]{0,1:T(8,128)(2,1)} fusion(bf16[1024,1464]{1,0:T(8,128)(2,1)} %gather_fusion, pred[1024]{0:T(1024)(128)(4,1)S(1)} %compare_and_fusion.1), kind=kLoop, calls=%fused_computation.9 | loop fusion | flops 1499136 | bytes 5997568 | tf_op jit(solution)/shard_map/jit(_take)/select_n | solution.py:54
  22.5 4.7 %copy.20 = bf16[1464,1024]{1,0:T(8,128)(2,1)} copy(bf16[1464,1024]{0,1:T(8,128)(2,1)} %select_bitcast_fusion) | data formatting | bytes 5996544 | tf_op jit(solution)/shard_map/jit(_take)/select_n | solution.py:54
  27.2 7.7 %copy.21 = bf16[3,488,1024]{1,0,2:T(4,128)(2,1)} copy(bf16[3,488,1024]{2,1,0:T(8,128)(2,1)} %bitcast.60) | data formatting | bytes 5996544 | tf_op jit(solution)/shard_map/reshape | solution.py:55
  34.8 0.0 copy-start.2
  34.8 0.0 copy-start
  34.8 11.1 %all-to-all-start = ((bf16[3,488,1024]{1,0,2:T(4,128)(2,1)}), bf16[3,488,1024]{1,0,2:T(4,128)(2,1)}, u32[]{:S(2)}, u32[]{:S(2)}) async-start(bf16[3,488,1024]{1,0,2:T(4,128)(2,1)} %copy.21), calls=%async_computation | async-start | bytes 8388608 | tf_op jit(solution)/shard_map/all_to_all | solution.py:56
  45.9 0.0 copy-done.2
  45.9 0.6 fusion.11
  46.5 0.0 copy-done
  48.0 0.0 collective-permute-done
  48.0 0.0 collective-permute-done.1
  48.1 0.8 select_add_fusion
  48.8 49.7 %all-to-all-done = bf16[3,488,1024]{1,0,2:T(4,128)(2,1)} async-done(((bf16[3,488,1024]{1,0,2:T(4,128)(2,1)}), bf16[3,488,1024]{1,0,2:T(4,128)(2,1)}, u32[]{:S(2)}, u32[]{:S(2)}) %all-to-all-start) | async-done | bytes 2998304 | tf_op jit(solution)/shard_map/all_to_all | solution.py:56
  98.5 7.5 %copy.22 = bf16[3,488,1024]{2,1,0:T(8,128)(2,1)} copy(bf16[3,488,1024]{1,0,2:T(4,128)(2,1)} %all-to-all-done) | data formatting | bytes 5996544 | tf_op jit(solution)/shard_map/all_to_all | solution.py:56
  106.0 4.6 %copy.23 = bf16[1464,1024]{0,1:T(8,128)(2,1)} copy(bf16[1464,1024]{1,0:T(8,128)(2,1)} %bitcast.61) | data formatting | bytes 5996544 | tf_op jit(solution)/shard_map/reshape | solution.py:57
  110.6 4.1 %maximum_maximum_fusion = bf16[1281,1464]{1,0:T(8,128)(2,1)} fusion(bf16[1024,1464]{1,0:T(8,128)(2,1)} %bitcast.59, bf16[256,1464]{1,0:T(8,128)(2,1)S(1)} %bitcast.58, bf16[1281]{0:T(1024)(128)(2,1)S(1)} %pad.2.clone), kind=kLoop, calls=%fused_computation.8 | loop fusion | flops 11252304 | bytes 7501170 | tf_op jit(solution)/shard_map/concatenate | solution.py:59
  114.8 58.0 %gather_fusion.1 = bf16[9216,1464]{1,0:T(8,128)(2,1)} fusion(bf16[1281,1464]{1,0:T(8,128)(2,1)} %maximum_maximum_fusion, s32[9216]{0:T(1024)S(1)} %broadcast_clamp_fusion), kind=kCustom, calls=%fused_computation.1 | custom fusion | bytes 54005760 | tf_op jit(solution)/shard_map/jit(_take)/gather | solution.py:61
  172.8 33.0 %copy.24 = bf16[9216,1464]{0,1:T(8,128)(2,1)} copy(bf16[9216,1464]{1,0:T(8,128)(2,1)} %gather_fusion.1) | data formatting | bytes 53968896 | tf_op jit(solution)/shard_map/jit(_take)/gather | solution.py:61
  205.7 39.9 %gather.12 = bf16[36,256,3,488]{1,0,3,2:T(8,128)(2,1)} reshape(bf16[9216,1464]{0,1:T(8,128)(2,1)} %copy.24) | data formatting | bytes 53968896 | tf_op jit(solution)/shard_map/jit(_take)/gather | solution.py:61
  245.6 20.4 %broadcast_select_fusion = bf16[36,256,3,488]{1,0,3,2:T(8,128)(2,1)} fusion(bf16[36,256,3,488]{1,0,3,2:T(8,128)(2,1)} %gather.12, pred[36,256]{1,0:T(8,128)(4,1)S(1)} %compare_and_fusion), kind=kLoop, calls=%fused_computation.2 | loop fusion | flops 13492224 | bytes 53978112 | tf_op jit(solution)/shard_map/jit(_take)/select_n | solution.py:61
  266.0 30.2 %fusion.5 = f32[3,488,256]{2,1,0:T(8,128)} fusion(bf16[36,488,488]{2,1,0:T(8,128)(2,1)} %param.9, bf16[36,256,3,488]{1,0,3,2:T(8,128)(2,1)} %broadcast_select_fusion, pred[256]{0:T(512)(128)(4,1)S(1)} %iota_compare_fusion), kind=kOutput, calls=%fused_computation.11 | convolution fusion | flops 13168785408 | bytes 45630208 | tf_op jit(solution)/shard_map/rij,rbcj->cib/dot_general | solution.py:63
  (16 shorter events, 0.2 us)
Async XLA Ops:
  2.8 10.2 %copy-start.1 = (s32[1,1024]{1,0:T(1,128)S(1)}, s32[1,1024]{1,0:T(1,128)}, u32[]{:S(2)}) copy-start(s32[1,1024]{1,0:T(1,128)} %param.12) | copy-start | bytes 12292
  6.2 41.8 %collective-permute-start = (f32[3,488,1]{1,2,0:T(1,128)S(1)}, f32[3,488,1]{1,2,0:T(1,128)S(1)}, u32[]{:S(2)}, u32[]{:S(2)}) collective-permute-start(f32[3,488,1]{1,2,0:T(1,128)S(1)} %dynamic-slice_bitcast_fusion), channel_id=1, source_target_pairs={{0,1},{1,2},{2,3},{3,4},{4,5},{5,6},{6,7},{7,8},{8,9},{9,10},{10,1... | collective-permute-start | bytes 17576 | tf_op jit(solution)/shard_map/ppermute | solution.py:15
  10.7 37.3 %collective-permute-start.1 = (f32[3,488,1]{1,2,0:T(1,128)S(1)}, f32[3,488,1]{1,2,0:T(1,128)S(1)}, u32[]{:S(2)}, u32[]{:S(2)}) collective-permute-start(f32[3,488,1]{1,2,0:T(1,128)S(1)} %slice.16), channel_id=1, source_target_pairs={{1,0},{2,1},{3,2},{4,3},{5,4},{6,5},{7,6},{8,7},{9,8},{10,9},{11,1... | collective-permute-start | bytes 17576 | tf_op jit(solution)/shard_map/ppermute | solution.py:17
  34.8 11.1 %copy-start.2 = (s32[1,2]{1,0:T(1,128)S(1)}, s32[1,2]{1,0:T(1,128)}, u32[]{:S(2)}) copy-start(s32[1,2]{1,0:T(1,128)} %param.11) | copy-start | bytes 28
  34.8 11.7 %copy-start = (s32[256,36]{0,1:T(8,128)S(1)}, s32[256,36]{0,1:T(8,128)}, u32[]{:S(2)}) copy-start(s32[256,36]{0,1:T(8,128)} %param.13) | copy-start | bytes 110596
  34.8 63.7 %all-to-all-start = ((bf16[3,488,1024]{1,0,2:T(4,128)(2,1)}), bf16[3,488,1024]{1,0,2:T(4,128)(2,1)}, u32[]{:S(2)}, u32[]{:S(2)}) async-start(bf16[3,488,1024]{1,0,2:T(4,128)(2,1)} %copy.21), calls=%async_computation | async-start | bytes 8388608 | tf_op jit(solution)/shard_map/all_to_all | solution.py:56
where the time goes:
time: 299 us; the launch traced here: 296 us
  local copies, waits for them, and re-layouts  162 us (54%)
  waiting for transfers between devices  49.7 us (17%)
  matrix products  33.6 us (11%)
  other arithmetic  30.5 us (10%)
  starting transfers between devices  17.5 us (6%)
    gather x3, local copies, waits for them, and re-layouts, body(): picked_rows = jnp.take(buffer_rows, vlist_cols.T.reshape(-1), axis=0)  131 us
    all_to_all x1, waiting for transfers between devices, body(): lax.all_to_all(outgoing, 'morton', split_axis=2, concat_axis=2, tiled=True)  49.7 us
    dot_general x1, matrix products, body(): jnp.einsum('rij,rbcj->cib', transfer_ops, picked_rows, preferred_element_...  30.2 us
    select_n x2, other arithmetic, body(): picked_rows = jnp.take(buffer_rows, vlist_cols.T.reshape(-1), axis=0)  20.5 us
    all_to_all x1, starting transfers between devices, body(): lax.all_to_all(outgoing, 'morton', split_axis=2, concat_axis=2, tiled=True)  11.1 us
    reshape x1, local copies, waits for them, and re-layouts, body(): outgoing_rows.T.reshape(channels, points, dev_count * ghost_total)  7.65 us
    all_to_all x1, local copies, waits for them, and re-layouts, body(): lax.all_to_all(outgoing, 'morton', split_axis=2, concat_axis=2, tiled=True)  7.46 us
  transfers between devices with their start and end apart: 3, of which 1 were waited for; matrix products, arithmetic and copies ran while one was open for 8% of the time, Pallas kernels for 0%

commit v1 on v0

v1 whole, which is shorter than its diff:
```python
import functools

import jax
import jax.numpy as jnp
from jax import lax
from jax.experimental import pallas as pl
from jax.experimental.pallas import tpu as pltpu
from jax.sharding import PartitionSpec as P

BOX = 16
LANES = 128
KPAD = 512
BF16 = jnp.bfloat16
F32 = jnp.float32


def pack_kernel(mult_ref, slots_ref, out_ref):
    channels, points, send_slots = mult_ref.shape
    ghosts = slots_ref.shape[1]
    box_ids = lax.broadcasted_iota(jnp.int32, (send_slots, ghosts), 0)
    onehot = jnp.where(box_ids == slots_ref[...], 1.0, 0.0).astype(BF16)
    for c in range(channels):
        rows = lax.dot_general(
            onehot, mult_ref[c], (((0,), (1,)), ((), ())), preferred_element_type=F32
        ).astype(BF16)
        rows = jnp.concatenate([rows, jnp.zeros((ghosts, KPAD - points), BF16)], axis=1)
        out_ref[:, c * KPAD : (c + 1) * KPAD] = rows


def pack(multipoles, send_slots):
    channels, points, slots = multipoles.shape
    ghosts = send_slots.shape[1]
    half = slots // 2
    return pl.pallas_call(
        pack_kernel,
        grid=(1,),
        in_specs=[
            pl.BlockSpec((channels, points, half), lambda i: (0, 0, 0)),
            pl.BlockSpec((1, ghosts), lambda i: (0, 0)),
        ],
        out_specs=pl.BlockSpec((ghosts, channels * KPAD), lambda i: (0, 0)),
        out_shape=jax.ShapeDtypeStruct((ghosts, channels * KPAD), BF16),
        compiler_params=pltpu.CompilerParams(vmem_limit_bytes=40 * 2**20),
    )(multipoles, send_slots)


def local_kernel(live_ref, mult_ref, out_ref):
    channels, points, slots = mult_ref.shape
    keep = lax.broadcasted_iota(jnp.int32, (slots, 1), 0) < live_ref[0]
    for c in range(channels):
        rows = jnp.where(keep, mult_ref[c].astype(F32).T, 0.0).astype(BF16)
        rows = jnp.concatenate([rows, jnp.zeros((slots, KPAD - points), BF16)], axis=1)
        out_ref[:, c * KPAD : (c + 1) * KPAD] = rows


def local_rows(live, multipoles):
    channels, points, slots = multipoles.shape
    return pl.pallas_call(
        local_kernel,
        in_specs=[
            pl.BlockSpec(memory_space=pltpu.SMEM),
            pl.BlockSpec(memory_space=pltpu.VMEM),
        ],
        out_specs=pl.BlockSpec(memory_space=pltpu.VMEM),
        out_shape=jax.ShapeDtypeStruct((slots, channels * KPAD), BF16),
        compiler_params=pltpu.CompilerParams(vmem_limit_bytes=40 * 2**20),
    )(live, multipoles)


def m2l_kernel(vl_ref, live_ref, arr_ref, loc_ref, t_ref, out_ref, src, g0, g1, acc, *, rel):
    slots = loc_ref.shape[0]
    ghosts = arr_ref.shape[0]
    channels, points, _ = out_ref.shape
    chunks = KPAD // LANES
    step = pl.program_id(0)

    def gather(r, dst):
        base = r * slots
        for t in range(slots):
            i = pl.multiple_of(vl_ref[base + t], BOX)
            dst[pl.ds(t * BOX, BOX), :] = src[pl.ds(i, BOX), :]

    def apply(k, got):
        for c in range(channels):
            x = jnp.concatenate(
                [got[pl.ds(c * chunks + q, slots, stride=BOX), :].astype(BF16) for q in range(chunks)],
                axis=1,
            )
            acc[c] += jnp.dot(x, t_ref[k], preferred_element_type=F32)

    @pl.when(step == 0)
    def _():
        def fill(ref, first):
            def one(b, carry):
                rows = ref[pl.ds(pl.multiple_of(b * 8, 8), 8), :].astype(F32)
                for q in range(channels * chunks):
                    src[pl.ds((first + b * 8) * BOX + q, 8, stride=BOX), :] = rows[:, q * LANES : (q + 1) * LANES]
                return carry

            lax.fori_loop(0, ref.shape[0] // 8, one, 0, unroll=4)

        fill(loc_ref, 0)
        fill(arr_ref, slots)
        src[pl.ds((slots + ghosts) * BOX, BOX), :] = jnp.zeros((BOX, LANES), F32)
        acc[...] = jnp.zeros_like(acc)
        gather(0, g0)

    gather(2 * step + 1, g1)
    apply(0, g0)
    gather(jnp.minimum(2 * step + 2, rel - 1), g0)
    apply(1, g1)

    @pl.when(step == pl.num_programs(0) - 1)
    def _():
        keep = lax.broadcasted_iota(jnp.int32, (1, slots), 1) < live_ref[0]
        for c in range(channels):
            out_ref[c] = jnp.where(keep, acc[c].T[:points], 0.0)


def m2l(cols, live, arrived, local, ops, channels, points):
    rel = ops.shape[0]
    ghosts = arrived.shape[0]
    slots = local.shape[0]
    width = channels * KPAD
    return pl.pallas_call(
        functools.partial(m2l_kernel, rel=rel),
        grid_spec=pltpu.PrefetchScalarGridSpec(
            num_scalar_prefetch=2,
            grid=(rel // 2,),
            in_specs=[
                pl.BlockSpec((ghosts, width), lambda i, *_: (0, 0)),
                pl.BlockSpec((slots, width), lambda i, *_: (0, 0)),
                pl.BlockSpec((2, KPAD, KPAD), lambda i, *_: (i, 0, 0)),
            ],
            out_specs=pl.BlockSpec((channels, points, slots), lambda i, *_: (0, 0, 0)),
            scratch_shapes=[
                pltpu.VMEM(((slots + ghosts + 8) * BOX, LANES), F32),
                pltpu.VMEM((slots * BOX, LANES), F32),
                pltpu.VMEM((slots * BOX, LANES), F32),
                pltpu.VMEM((channels, slots, KPAD), F32),
            ],
        ),
        out_shape=jax.ShapeDtypeStruct((channels, points, slots), F32),
        compiler_params=pltpu.CompilerParams(vmem_limit_bytes=50 * 2**20),
    )(cols, live, arrived, local, ops)


def shifted(cells, step):
    count = lax.axis_size("morton")
    if step > 0:
        pairs = [(i, i + 1) for i in range(count - 1)]
    else:
        pairs = [(i + 1, i) for i in range(count - 1)]
    return lax.ppermute(cells, "morton", pairs)


def body(multipoles, upward_ops, transfer_ops, live_counts, seam_joins, send_slots, vlist_cols):
    channels, points, slot_total = multipoles.shape
    group_total = slot_total // 8
    dev_count = lax.axis_size("morton")
    ghosts = send_slots.shape[1]
    width = channels * KPAD
    outgoing = pack(multipoles, send_slots)
    outgoing, multipoles = lax.optimization_barrier((outgoing, multipoles))
    arrived = lax.all_to_all(
        outgoing.reshape(dev_count, ghosts // dev_count, width), "morton", 0, 0, tiled=True
    ).reshape(ghosts, width)

    local = local_rows(live_counts, multipoles)
    ops = jnp.pad(jnp.swapaxes(transfer_ops, 1, 2), ((0, 0), (0, KPAD - points), (0, KPAD - points)))
    cols = (vlist_cols.T * BOX).reshape(-1)

    slot_ids = jnp.arange(slot_total, dtype=jnp.int32)
    keep = (slot_ids < live_counts[0])[None, None, :]
    masked = jnp.where(keep, multipoles, jnp.zeros_like(multipoles))
    children = masked.reshape(channels, points, group_total, 8)
    partial_value = jnp.einsum("oij,cjgo->cig", upward_ops, children, preferred_element_type=F32)
    last_group = (live_counts[0] - 1) // 8
    last_part = lax.dynamic_slice_in_dim(partial_value, last_group, 1, 2)[:, :, 0]
    from_left = shifted(last_part, 1)
    from_right = shifted(partial_value[:, :, 0], -1)
    group_ids = jnp.arange(group_total, dtype=jnp.int32)
    joins = seam_joins[0].astype(F32)
    parent_mult = partial_value + jnp.where(
        (group_ids == 0)[None, None, :], (joins[0] * from_left)[:, :, None], F32(0.0)
    )
    parent_mult = parent_mult + jnp.where(
        (group_ids == last_group)[None, None, :], (joins[1] * from_right)[:, :, None], F32(0.0)
    )
    local_check = m2l(cols, live_counts, arrived, local, ops, channels, points)
    return (local_check, parent_mult)


def solution(mesh):
    placed = (
        P(None, None, "morton"),
        P(),
        P(),
        P("morton"),
        P("morton", None),
        P("morton", None),
        P("morton", None),
    )
    return jax.shard_map(
        body,
        mesh=mesh,
        in_specs=placed,
        out_specs=(P(None, None, "morton"), P(None, None, "morton")),
        check_vma=False,
    )
```

time: 299 us -> 121 us (0.40)
  the two profiles are of different devices: /device:TPU:1 before, /device:TPU:111 now
where the time goes in v1:
time: 121 us; the launch traced here: 120 us
  local copies, waits for them, and re-layouts  50 us (41%)
  Pallas kernels  41.5 us (34%)
  starting transfers between devices  19.9 us (16%)
  matrix products  3.43 us (3%)
  other arithmetic  3.36 us (3%)
  between operations  1.48 us (1%)
    pallas_call x1, Pallas kernels, m2l(): pl.pallas_call(functools.partial(m2l_kernel, rel=rel), grid_spec=pltpu.Pr...  40.2 us
    unnamed x19, local copies, waits for them, and re-layouts  30.3 us
    pad x1, local copies, waits for them, and re-layouts, body(): jnp.pad(jnp.swapaxes(transfer_ops, 1, 2), ((0, 0), (0, KPAD - points), (0...  16.8 us
    all_to_all x1, starting transfers between devices, body(): lax.all_to_all(outgoing.reshape(dev_count, ghosts // dev_count, width), '...  10.1 us
    ppermute x2, starting transfers between devices, shifted(): return lax.ppermute(cells, 'morton', pairs)  9.78 us
    dot_general x1, matrix products, body(): jnp.einsum('oij,cjgo->cig', upward_ops, children, preferred_element_type=...  3.43 us
  transfers between devices with their start and end apart: 3, of which 0 were waited for; matrix products, arithmetic and copies ran while one was open for 42% of the time, Pallas kernels for 0%

profile of v1, /device:TPU:111, one launch (start us, length us, event | category | flops | bytes accessed | tf_op | source)
XLA Modules:
  0.0 119.7 jit_solution(6338383846896903719)
XLA Ops:
  0.6 0.0 copy-start.1
  0.6 1.1 copy-done.1
  1.8 0.0 copy-start.5
  1.8 0.7 copy-done.5
  2.4 1.1 shard_map.86
  3.5 0.0 copy-start
  3.5 1.7 %copy-done = bf16[1024,1536]{1,0:T(8,128)(2,1)} copy-done((bf16[1024,1536]{1,0:T(8,128)(2,1)}, bf16[1024,1536]{1,0:T(8,128)(2,1)S(1)}, u32[]{:S(2)}) %copy-start) | copy-done | bytes 3145752
  5.2 10.1 %all-to-all-start = ((bf16[128,8,1536]{2,1,0:T(8,128)(2,1)}), bf16[128,8,1536]{2,1,0:T(8,128)(2,1)S(1)}, u32[]{:S(2)}, u32[]{:S(2)}) async-start(bf16[128,8,1536]{2,1,0:T(8,128)(2,1)} %bitcast.27), calls=%async_computation | async-start | bytes 6291456 | tf_op jit(solution)/shard_map/all_to_all | solution.py:165
  15.9 2.3 %copy.12 = bf16[3,488,256]{1,2,0:T(8,128)(2,1)} copy(bf16[3,488,256]{2,1,0:T(8,128)(2,1)} %mult_ref.2) | data formatting | bytes 1499136 | tf_op jit(solution)/shard_map/optimization_barrier | solution.py:164
  18.2 0.0 copy-start.7
  18.2 1.3 %select_bitcast_fusion = bf16[3,488,32,8]{1,3,2,0:T(8,128)(2,1)S(1)} fusion(bf16[3,488,256]{1,2,0:T(8,128)(2,1)} %copy.12, pred[256]{0:T(512)(128)(4,1)S(1)} %iota_compare_fusion), kind=kLoop, calls=%fused_computation.3 | loop fusion | flops 374784 | bytes 1499392 | tf_op jit(solution)/shard_map/reshape | solution.py:176
  19.5 3.4 %fusion = f32[3,32,488,1]{2,1,3,0:T(8,128)S(1)} fusion(bf16[8,488,488]{2,1,0:T(8,128)(2,1)} %param.8, bf16[3,488,32,8]{1,3,2,0:T(8,128)(2,1)S(1)} %select_bitcast_fusion), kind=kOutput, calls=%fused_computation | convolution fusion | flops 365789184 | bytes 4747264 | tf_op jit(solution)/shard_map/oij,cjgo->cig/dot_general | solution.py:177
  23.0 2.3 %collective-permute-start.1 = (f32[3,488]{1,0:T(4,128)S(1)}, f32[3,488]{1,0:T(4,128)S(1)}, u32[]{:S(2)}, u32[]{:S(2)}) collective-permute-start(f32[3,488]{1,0:T(4,128)S(1)} %bitcast.31), channel_id=1, source_target_pairs={{1,0},{2,1},{3,2},{4,3},{5,4},{6,5},{7,6},{8,7},{9,8},{10,9},{11,1... | collective-permute-start | bytes 17576 | tf_op jit(solution)/shard_map/ppermute | solution.py:154
  25.3 7.5 %collective-permute-start = (f32[3,488]{1,0:T(4,128)S(1)}, f32[3,488]{1,0:T(4,128)S(1)}, u32[]{:S(2)}, u32[]{:S(2)}) collective-permute-start(f32[3,488]{1,0:T(4,128)S(1)} %bitcast.32), channel_id=1, source_target_pairs={{0,1},{1,2},{2,3},{3,4},{4,5},{5,6},{6,7},{7,8},{8,9},{9,10},{10,1... | collective-permute-start | bytes 17576 | tf_op jit(solution)/shard_map/ppermute | solution.py:154
  32.8 0.0 copy-done.7
  32.8 0.6 fusion.3
  33.4 0.0 copy-done.6
  33.5 0.0 copy-start.2
  33.5 1.1 copy-done.2
  34.6 0.3 shard_map.87.loc_ref
  34.9 0.0 copy-start.3
  34.9 0.9 copy-done.3
  35.8 23.7 %copy.11 = bf16[36,488,488]{1,2,0:T(8,128)(2,1)} copy(bf16[36,488,488]{2,1,0:T(8,128)(2,1)} %param.9) | data formatting | bytes 34292736 | tf_op args[2]
  59.5 16.8 %pad.4.t_ref = bf16[36,512,512]{2,1,0:T(8,128)(2,1)} pad(bf16[36,488,488]{2,1,0:T(8,128)(2,1)} %bitcast.28, bf16[]{:T(256)} %constant.21.clone.1), padding=0_0x0_24x0_24 | pad | bytes 36020736 | tf_op jit(solution)/shard_map/jit(_pad)/pad | solution.py:170
  76.3 0.0 collective-permute-done.1
  76.3 0.6 broadcast_multiply_fusion
  76.9 0.0 collective-permute-done
  77.0 0.7 broadcast_multiply_fusion.1
  77.6 0.8 select_add_fusion
  78.4 0.0 all-to-all-done
  78.4 1.1 copy-done.4
  79.5 40.2 %shard_map.88 = f32[3,488,256]{2,1,0:T(8,128)} custom-call(s32[9216]{0:T(1024)S(1)} %reshape.37.vl_ref, s32[1]{0:T(128)} %copy.23.live_ref, bf16[1024,1536]{1,0:T(8,128)(2,1)S(1)} %bitcast.26, bf16[256,1536]{1,0:T(8,128)(2,1)S(1)} %copy-done.4, bf16[36,512,512]{2,1,0:T(8,128)(2,1)} %pad.4.t_ref), custom_call_target="tpu_custom_call" | custom-call | tf_op jit(solution)/shard_map/pallas_call | solution.py:125
  (11 shorter events, 0.1 us)
Async XLA Ops:
  0.6 1.1 copy-start.1
  1.8 0.7 copy-start.5
  3.5 1.7 %copy-start = (bf16[1024,1536]{1,0:T(8,128)(2,1)}, bf16[1024,1536]{1,0:T(8,128)(2,1)S(1)}, u32[]{:S(2)}) copy-start(bf16[1024,1536]{1,0:T(8,128)(2,1)S(1)} %shard_map.86) | copy-start | bytes 9437188
  5.2 73.2 %all-to-all-start = ((bf16[128,8,1536]{2,1,0:T(8,128)(2,1)}), bf16[128,8,1536]{2,1,0:T(8,128)(2,1)S(1)}, u32[]{:S(2)}, u32[]{:S(2)}) async-start(bf16[128,8,1536]{2,1,0:T(8,128)(2,1)} %bitcast.27), calls=%async_computation | async-start | bytes 6291456 | tf_op jit(solution)/shard_map/all_to_all | solution.py:165
  18.2 14.6 %copy-start.7 = (s32[1,2]{1,0:T(1,128)S(1)}, s32[1,2]{1,0:T(1,128)}, u32[]{:S(2)}) copy-start(s32[1,2]{1,0:T(1,128)} %param.11) | copy-start | bytes 28
  18.2 15.2 %copy-start.6 = (s32[256,36]{0,1:T(8,128)S(1)}, s32[256,36]{0,1:T(8,128)}, u32[]{:S(2)}) copy-start(s32[256,36]{0,1:T(8,128)} %param.13) | copy-start | bytes 110596
  23.0 53.3 %collective-permute-start.1 = (f32[3,488]{1,0:T(4,128)S(1)}, f32[3,488]{1,0:T(4,128)S(1)}, u32[]{:S(2)}, u32[]{:S(2)}) collective-permute-start(f32[3,488]{1,0:T(4,128)S(1)} %bitcast.31), channel_id=1, source_target_pairs={{1,0},{2,1},{3,2},{4,3},{5,4},{6,5},{7,6},{8,7},{9,8},{10,9},{11,1... | collective-permute-start | bytes 17576 | tf_op jit(solution)/shard_map/ppermute | solution.py:154
  25.3 51.7 %collective-permute-start = (f32[3,488]{1,0:T(4,128)S(1)}, f32[3,488]{1,0:T(4,128)S(1)}, u32[]{:S(2)}, u32[]{:S(2)}) collective-permute-start(f32[3,488]{1,0:T(4,128)S(1)} %bitcast.32), channel_id=1, source_target_pairs={{0,1},{1,2},{2,3},{3,4},{4,5},{5,6},{6,7},{7,8},{8,9},{9,10},{10,1... | collective-permute-start | bytes 17576 | tf_op jit(solution)/shard_map/ppermute | solution.py:154
  33.5 1.1 copy-start.2
  34.9 0.9 copy-start.3
  78.4 1.1 copy-start.4

commit v2 on v1

--- a/solution.py
+++ b/solution.py
@@ -7,7 +7,7 @@
 from jax.experimental.pallas import tpu as pltpu
 from jax.sharding import PartitionSpec as P
 
-BOX = 16
+BOX = 12
 LANES = 128
 KPAD = 512
 BF16 = jnp.bfloat16
@@ -67,81 +67,144 @@
     )(live, multipoles)
 
 
-def m2l_kernel(vl_ref, live_ref, arr_ref, loc_ref, t_ref, out_ref, src, g0, g1, acc, *, rel):
+def ops_kernel(t_ref, out_ref):
+    points = t_ref.shape[1]
+    out_ref[...] = jnp.zeros_like(out_ref)
+    for k in range(t_ref.shape[0]):
+        out_ref[k, :points, :points] = t_ref[k].astype(F32).T.astype(BF16)
+
+
+def padded_ops(ops, count):
+    rel, points, _ = ops.shape
+    return pl.pallas_call(
+        ops_kernel,
+        grid=(rel // count,),
+        in_specs=[pl.BlockSpec((count, points, points), lambda i: (i, 0, 0))],
+        out_specs=pl.BlockSpec((count, KPAD, KPAD), lambda i: (i, 0, 0)),
+        out_shape=jax.ShapeDtypeStruct((rel, KPAD, KPAD), BF16),
+        compiler_params=pltpu.CompilerParams(vmem_limit_bytes=16 * 2**20),
+    )(ops)
+
+
+def m2l_kernel(
+    vl_ref, live_ref, arr_hbm, loc_hbm, t_hbm, out_ref, buf, acc, arr_ref, loc_ref, t_ref, loc_sem, arr_sem, t_sem, *, depth, batch
+):
     slots = loc_ref.shape[0]
     ghosts = arr_ref.shape[0]
+    parts = arr_sem.shape[0]
+    span = ghosts // parts
     channels, points, _ = out_ref.shape
     chunks = KPAD // LANES
-    step = pl.program_id(0)
-
-    def gather(r, dst):
+    groups = t_hbm.shape[0] // depth
+    laps = groups // 2
+    first = (slots + ghosts + 4) * BOX
+
+    def start(p):
+        return first + p * slots * BOX
+
+    def gather(r, p, t0, t1):
         base = r * slots
-        for t in range(slots):
-            i = pl.multiple_of(vl_ref[base + t], BOX)
-            dst[pl.ds(t * BOX, BOX), :] = src[pl.ds(i, BOX), :]
-
-    def apply(k, got):
+        for tb in range(t0, t1, batch):
+            held = []
+            for t in range(tb, tb + batch):
+                i = vl_ref[base + t]
+                held.append((start(p) + t * BOX, buf[pl.ds(i, 8), :], buf[pl.ds(i + 8, BOX - 8), :]))
+            for to, head, tail in held:
+                buf[pl.ds(to, 8), :] = head
+                buf[pl.ds(to + 8, BOX - 8), :] = tail
+
+    def ops_copy(lap):
+        place = lax.rem(lap, 2)
+        return pltpu.make_async_copy(t_hbm.at[pl.ds(lap * 2 * depth, 2 * depth)], t_ref.at[place], t_sem.at[place])
+
+    def part_copy(k):
+        rows = pl.ds(k * span, span)
+        return pltpu.make_async_copy(arr_hbm.at[rows], arr_ref.at[rows], arr_sem.at[k])
+
+    def fill(ref, low, count, at):
+        def one(b, carry):
+            rows = ref[pl.ds(pl.multiple_of(low + b * 16, 16), 16), :].astype(F32)
+            for q in range(BOX):
+                buf[pl.ds((at + b * 16) * BOX + q, 16, stride=BOX), :] = rows[:, q * LANES : (q + 1) * LANES]
+            return carry
+
+        lax.fori_loop(0, count // 16, one, 0, unroll=2)
+
+    loc_copy = pltpu.make_async_copy(loc_hbm, loc_ref, loc_sem)
+    loc_copy.start()
+    for k in range(parts):
+        part_copy(k).start()
+    ops_copy(0).start()
+    loc_copy.wait()
+    fill(loc_ref, 0, slots, 0)
+    for k in range(parts):
+        part_copy(k).wait()
+        fill(arr_ref, k * span, span, slots + k * span)
+    buf[pl.ds((slots + ghosts) * BOX, 16), :] = jnp.zeros((16, LANES), F32)
+    acc[...] = jnp.zeros_like(acc)
+    for p in range(depth):
+        gather(p, p, 0, slots)
+
+    def group(s, slot, place):
+        later = jnp.minimum(s + 1, groups - 1)
+        total = depth * slots
+        cuts = [total * c // channels // batch * batch for c in range(channels + 1)]
         for c in range(channels):
+            for p in range(depth):
+                lo, hi = max(cuts[c] - p * slots, 0), min(cuts[c + 1] - p * slots, slots)
+                if lo < hi:
+                    gather(later * depth + p, (1 - slot) * depth + p, lo, hi)
             x = jnp.concatenate(
-                [got[pl.ds(c * chunks + q, slots, stride=BOX), :].astype(BF16) for q in range(chunks)],
+                [
+                    buf[pl.ds(start(slot * depth + p) + c * chunks + q, slots, stride=BOX), :].astype(BF16)
+                    for p in range(depth)
+                    for q in range(chunks)
+                ],
                 axis=1,
             )
-            acc[c] += jnp.dot(x, t_ref[k], preferred_element_type=F32)
-
-    @pl.when(step == 0)
-    def _():
-        def fill(ref, first):
-            def one(b, carry):
-                rows = ref[pl.ds(pl.multiple_of(b * 8, 8), 8), :].astype(F32)
-                for q in range(channels * chunks):
-                    src[pl.ds((first + b * 8) * BOX + q, 8, stride=BOX), :] = rows[:, q * LANES : (q + 1) * LANES]
-                return carry
-
-            lax.fori_loop(0, ref.shape[0] // 8, one, 0, unroll=4)
-
-        fill(loc_ref, 0)
-        fill(arr_ref, slots)
-        src[pl.ds((slots + ghosts) * BOX, BOX), :] = jnp.zeros((BOX, LANES), F32)
-        acc[...] = jnp.zeros_like(acc)
-        gather(0, g0)
-
-    gather(2 * step + 1, g1)
-    apply(0, g0)
-    gather(jnp.minimum(2 * step + 2, rel - 1), g0)
-    apply(1, g1)
-
-    @pl.when(step == pl.num_programs(0) - 1)
-    def _():
-        keep = lax.broadcasted_iota(jnp.int32, (1, slots), 1) < live_ref[0]
-        for c in range(channels):
-            out_ref[c] = jnp.where(keep, acc[c].T[:points], 0.0)
+            w = t_ref[place, slot * depth : (slot + 1) * depth].reshape(depth * KPAD, KPAD)
+            acc[c] += jnp.dot(x, w, preferred_element_type=F32)
+
+    def lap(s, carry):
+        place = lax.rem(s, 2)
+        ops_copy(s).wait()
+
+        @pl.when(s + 1 < laps)
+        def _():
+            ops_copy(s + 1).start()
+
+        group(2 * s, 0, place)
+        group(2 * s + 1, 1, place)
+        return carry
+
+    lax.fori_loop(0, laps, lap, 0)
+    keep = lax.broadcasted_iota(jnp.int32, (1, slots), 1) < live_ref[0]
+    for c in range(channels):
+        out_ref[c] = jnp.where(keep, acc[c].T[:points], 0.0)
 
 
 def m2l(cols, live, arrived, local, ops, channels, points):
-    rel = ops.shape[0]
     ghosts = arrived.shape[0]
     slots = local.shape[0]
-    width = channels * KPAD
-    return pl.pallas_call(
-        functools.partial(m2l_kernel, rel=rel),
-        grid_spec=pltpu.PrefetchScalarGridSpec(
-            num_scalar_prefetch=2,
-            grid=(rel // 2,),
-            in_specs=[
-                pl.BlockSpec((ghosts, width), lambda i, *_: (0, 0)),
-                pl.BlockSpec((slots, width), lambda i, *_: (0, 0)),
-                pl.BlockSpec((2, KPAD, KPAD), lambda i, *_: (i, 0, 0)),
-            ],
-            out_specs=pl.BlockSpec((channels, points, slots), lambda i, *_: (0, 0, 0)),
-            scratch_shapes=[
-                pltpu.VMEM(((slots + ghosts + 8) * BOX, LANES), F32),
-                pltpu.VMEM((slots * BOX, LANES), F32),
-                pltpu.VMEM((slots * BOX, LANES), F32),
-                pltpu.VMEM((channels, slots, KPAD), F32),
-            ],
-        ),
+    depth = 2
+    smem = pl.BlockSpec(memory_space=pltpu.SMEM)
+    hbm = pl.BlockSpec(memory_space=pl.ANY)
+    return pl.pallas_call(
+        functools.partial(m2l_kernel, depth=depth, batch=16),
+        in_specs=[smem, smem, hbm, hbm, hbm],
+        out_specs=pl.BlockSpec(memory_space=pltpu.VMEM),
+        scratch_shapes=[
+            pltpu.VMEM(((slots + ghosts + 4 + 2 * depth * slots) * BOX, LANES), F32),
+            pltpu.VMEM((channels, slots, KPAD), F32),
+            pltpu.VMEM(arrived.shape, BF16),
+            pltpu.VMEM(local.shape, BF16),
+            pltpu.VMEM((2, 2 * depth, KPAD, KPAD), BF16),
+            pltpu.SemaphoreType.DMA,
+            pltpu.SemaphoreType.DMA((4,)),
+            pltpu.SemaphoreType.DMA((2,)),
+        ],
         out_shape=jax.ShapeDtypeStruct((channels, points, slots), F32),
-        compiler_params=pltpu.CompilerParams(vmem_limit_bytes=50 * 2**20),
+        compiler_params=pltpu.CompilerParams(vmem_limit_bytes=56 * 2**20),
     )(cols, live, arrived, local, ops)
 
 
@@ -161,13 +224,13 @@
     ghosts = send_slots.shape[1]
     width = channels * KPAD
     outgoing = pack(multipoles, send_slots)
-    outgoing, multipoles = lax.optimization_barrier((outgoing, multipoles))
+    outgoing, multipoles, transfer_ops = lax.optimization_barrier((outgoing, multipoles, transfer_ops))
     arrived = lax.all_to_all(
         outgoing.reshape(dev_count, ghosts // dev_count, width), "morton", 0, 0, tiled=True
     ).reshape(ghosts, width)
 
     local = local_rows(live_counts, multipoles)
-    ops = jnp.pad(jnp.swapaxes(transfer_ops, 1, 2), ((0, 0), (0, KPAD - points), (0, KPAD - points)))
+    ops = padded_ops(transfer_ops, 2)
     cols = (vlist_cols.T * BOX).reshape(-1)
 
     slot_ids = jnp.arange(slot_total, dtype=jnp.int32)

time: 121 us -> 87.7 us (0.72)
  the two profiles are of different devices: /device:TPU:111 before, /device:TPU:1 now
where the time goes in v2:
time: 87.7 us; the launch traced here: 87.2 us
  Pallas kernels  38 us (43%)
  starting transfers between devices  17.5 us (20%)
  local copies, waits for them, and re-layouts  16.8 us (19%)
  waiting for transfers between devices  7.86 us (9%)
  matrix products  3.38 us (4%)
  other arithmetic  2.22 us (3%)
  between operations  1.51 us (2%)
    pallas_call x1, Pallas kernels, m2l(): pl.pallas_call(functools.partial(m2l_kernel, depth=depth, batch=16), in_s...  28.6 us
    unnamed x18, local copies, waits for them, and re-layouts  15.3 us
    all_to_all x1, starting transfers between devices, body(): lax.all_to_all(outgoing.reshape(dev_count, ghosts // dev_count, width), '...  11.9 us
    pallas_call x1, Pallas kernels, padded_ops(): pl.pallas_call(ops_kernel, grid=(rel // count,), in_specs=[pl.BlockSpec((...  6.32 us
    ppermute x2, starting transfers between devices, shifted(): return lax.ppermute(cells, 'morton', pairs)  5.56 us
    all_to_all x1, waiting for transfers between devices, body(): lax.all_to_all(outgoing.reshape(dev_count, ghosts // dev_count, width), '...  3.95 us
    ppermute x2, waiting for transfers between devices, shifted(): return lax.ppermute(cells, 'morton', pairs)  3.91 us
    dot_general x1, matrix products, body(): jnp.einsum('oij,cjgo->cig', upward_ops, children, preferred_element_type=...  3.38 us
  transfers between devices with their start and end apart: 3, of which 2 were waited for; matrix products, arithmetic and copies ran while one was open for 8% of the time, Pallas kernels for 8%

profile of v2, /device:TPU:1, one launch (start us, length us, event | category | flops | bytes accessed | tf_op | source)
XLA Modules:
  0.0 87.2 jit_solution(18323542411733710153)
XLA Ops:
  0.6 0.0 copy-start.2
  0.6 1.1 %copy-done.2 = bf16[3,488,256]{2,1,0:T(8,128)(2,1)S(1)} copy-done((bf16[3,488,256]{2,1,0:T(8,128)(2,1)S(1)}, bf16[3,488,256]{2,1,0:T(8,128)(2,1)}, u32[]{:S(2)}) %copy-start.2) | copy-done | bytes 749592
  1.8 0.0 copy-start.5
  1.8 0.7 copy-done.5
  2.4 2.7 %shard_map.86 = bf16[1024,1536]{1,0:T(8,128)(2,1)} custom-call(bf16[3,488,256]{2,1,0:T(8,128)(2,1)S(1)} %copy-done.2, s32[1,1024]{1,0:T(1,128)S(1)} %copy-done.5), custom_call_target="tpu_custom_call" | custom-call | tf_op jit(solution)/shard_map/pallas_call | solution.py:34
  5.2 11.9 %all-to-all-start = ((bf16[128,8,1536]{2,1,0:T(8,128)(2,1)}), bf16[128,8,1536]{2,1,0:T(8,128)(2,1)}, u32[]{:S(2)}, u32[]{:S(2)}) async-start(bf16[128,8,1536]{2,1,0:T(8,128)(2,1)} %bitcast.1), calls=%async_computation | async-start | bytes 6291456 | tf_op jit(solution)/shard_map/all_to_all | solution.py:228
  17.7 0.0 copy-done.3
  17.7 0.3 copy.10
  18.0 0.0 copy-start.7
  18.0 0.0 copy-start.6
  18.1 0.1 select_bitcast_fusion
  18.2 3.4 %fusion = f32[3,32,488,1]{2,1,3,0:T(8,128)S(1)} fusion(bf16[8,488,488]{2,1,0:T(8,128)(2,1)} %param.8, bf16[3,488,32,8]{1,3,2,0:T(8,128)(2,1)S(1)} %select_bitcast_fusion), kind=kOutput, calls=%fused_computation | convolution fusion | flops 365789184 | bytes 4747264 | tf_op jit(solution)/shard_map/oij,cjgo->cig/dot_general | solution.py:240
  21.6 3.0 %collective-permute-start.1 = (f32[3,488]{1,0:T(4,128)S(1)}, f32[3,488]{1,0:T(4,128)S(1)}, u32[]{:S(2)}, u32[]{:S(2)}) collective-permute-start(f32[3,488]{1,0:T(4,128)S(1)} %bitcast.27), channel_id=1, source_target_pairs={{1,0},{2,1},{3,2},{4,3},{5,4},{6,5},{7,6},{8,7},{9,8},{10,9},{11,1... | collective-permute-start | bytes 17576 | tf_op jit(solution)/shard_map/ppermute | solution.py:217
  24.7 2.5 %collective-permute-start = (f32[3,488]{1,0:T(4,128)S(1)}, f32[3,488]{1,0:T(4,128)S(1)}, u32[]{:S(2)}, u32[]{:S(2)}) collective-permute-start(f32[3,488]{1,0:T(4,128)S(1)} %bitcast.28), channel_id=1, source_target_pairs={{0,1},{1,2},{2,3},{3,4},{4,5},{5,6},{6,7},{7,8},{8,9},{9,10},{10,1... | collective-permute-start | bytes 17576 | tf_op jit(solution)/shard_map/ppermute | solution.py:217
  27.2 0.0 copy-done.7
  27.3 0.6 fusion.3
  27.8 0.0 copy-done.6
  27.9 0.3 shard_map.87.loc_hbm
  28.2 0.0 copy-start.4
  28.2 1.0 %copy-done.4 = bf16[256,1536]{1,0:T(8,128)(2,1)} copy-done((bf16[256,1536]{1,0:T(8,128)(2,1)}, bf16[256,1536]{1,0:T(8,128)(2,1)S(1)}, u32[]{:S(2)}) %copy-start.4) | copy-done | bytes 786456
  29.1 0.6 reshape.37.vl_ref
  29.7 6.1 %copy-done.1 = bf16[36,488,488]{2,1,0:T(8,128)(2,1)S(1)} copy-done((bf16[36,488,488]{2,1,0:T(8,128)(2,1)S(1)}, bf16[36,488,488]{2,1,0:T(8,128)(2,1)}, u32[]{:S(2)}) %copy-start.1) | copy-done | bytes 17146392
  35.8 6.3 %shard_map.88.t_hbm = bf16[36,512,512]{2,1,0:T(8,128)(2,1)S(1)} custom-call(bf16[36,488,488]{2,1,0:T(8,128)(2,1)S(1)} %copy-done.1), custom_call_target="tpu_custom_call" | custom-call | tf_op jit(solution)/shard_map/pallas_call | solution.py:79
  42.2 0.0 copy-start
  42.2 6.4 %copy-done = bf16[36,512,512]{2,1,0:T(8,128)(2,1)} copy-done((bf16[36,512,512]{2,1,0:T(8,128)(2,1)}, bf16[36,512,512]{2,1,0:T(8,128)(2,1)S(1)}, u32[]{:S(2)}) %copy-start) | copy-done | bytes 18874392
  48.6 3.9 %collective-permute-done.1 = f32[3,488]{1,0:T(4,128)S(1)} collective-permute-done((f32[3,488]{1,0:T(4,128)S(1)}, f32[3,488]{1,0:T(4,128)S(1)}, u32[]{:S(2)}, u32[]{:S(2)}) %collective-permute-start.1) | collective-permute-done | bytes 5888 | tf_op jit(solution)/shard_map/ppermute | solution.py:217
  52.5 0.6 broadcast_multiply_fusion
  53.2 0.0 collective-permute-done
  53.2 0.7 broadcast_multiply_fusion.1
  53.9 0.8 select_add_fusion
  54.6 4.0 %all-to-all-done = bf16[128,8,1536]{2,1,0:T(8,128)(2,1)} async-done(((bf16[128,8,1536]{2,1,0:T(8,128)(2,1)}), bf16[128,8,1536]{2,1,0:T(8,128)(2,1)}, u32[]{:S(2)}, u32[]{:S(2)}) %all-to-all-start) | async-done | bytes 3145760 | tf_op jit(solution)/shard_map/all_to_all | solution.py:228
  58.6 28.6 %shard_map.89 = f32[3,488,256]{2,1,0:T(8,128)} custom-call(s32[9216]{0:T(1024)} %reshape.37.vl_ref, s32[1]{0:T(128)} %copy.21.live_ref, bf16[1024,1536]{1,0:T(8,128)(2,1)} %bitcast.2.arr_hbm, bf16[256,1536]{1,0:T(8,128)(2,1)} %copy-done.4, bf16[36,512,512]{2,1,0:T(8,128)(2,1)} %copy-done), custom_call_target="tpu_custom_call" | custom-call | tf_op jit(solution)/shard_map/pallas_call | solution.py:192
  (10 shorter events, 0.0 us)
Async XLA Ops:
  0.6 1.1 %copy-start.2 = (bf16[3,488,256]{2,1,0:T(8,128)(2,1)S(1)}, bf16[3,488,256]{2,1,0:T(8,128)(2,1)}, u32[]{:S(2)}) copy-start(bf16[3,488,256]{2,1,0:T(8,128)(2,1)} %mult_ref.2) | copy-start | bytes 2248708
  1.8 0.7 copy-start.5
  5.2 12.6 %copy-start.3 = (bf16[3,488,256]{2,1,0:T(8,128)(2,1)S(1)}, bf16[3,488,256]{2,1,0:T(8,128)(2,1)}, u32[]{:S(2)}) copy-start(bf16[3,488,256]{2,1,0:T(8,128)(2,1)} %mult_ref.2) | copy-start | bytes 2248708
  5.2 53.4 %all-to-all-start = ((bf16[128,8,1536]{2,1,0:T(8,128)(2,1)}), bf16[128,8,1536]{2,1,0:T(8,128)(2,1)}, u32[]{:S(2)}, u32[]{:S(2)}) async-start(bf16[128,8,1536]{2,1,0:T(8,128)(2,1)} %bitcast.1), calls=%async_computation | async-start | bytes 6291456 | tf_op jit(solution)/shard_map/all_to_all | solution.py:228
  18.0 9.2 %copy-start.7 = (s32[1,2]{1,0:T(1,128)S(1)}, s32[1,2]{1,0:T(1,128)}, u32[]{:S(2)}) copy-start(s32[1,2]{1,0:T(1,128)} %param.11) | copy-start | bytes 28
  18.0 9.8 %copy-start.6 = (s32[256,36]{0,1:T(8,128)S(1)}, s32[256,36]{0,1:T(8,128)}, u32[]{:S(2)}) copy-start(s32[256,36]{0,1:T(8,128)} %param.13) | copy-start | bytes 110596
  21.6 30.9 %collective-permute-start.1 = (f32[3,488]{1,0:T(4,128)S(1)}, f32[3,488]{1,0:T(4,128)S(1)}, u32[]{:S(2)}, u32[]{:S(2)}) collective-permute-start(f32[3,488]{1,0:T(4,128)S(1)} %bitcast.27), channel_id=1, source_target_pairs={{1,0},{2,1},{3,2},{4,3},{5,4},{6,5},{7,6},{8,7},{9,8},{10,9},{11,1... | collective-permute-start | bytes 17576 | tf_op jit(solution)/shard_map/ppermute | solution.py:217
  24.7 28.5 %collective-permute-start = (f32[3,488]{1,0:T(4,128)S(1)}, f32[3,488]{1,0:T(4,128)S(1)}, u32[]{:S(2)}, u32[]{:S(2)}) collective-permute-start(f32[3,488]{1,0:T(4,128)S(1)} %bitcast.28), channel_id=1, source_target_pairs={{0,1},{1,2},{2,3},{3,4},{4,5},{5,6},{6,7},{7,8},{8,9},{9,10},{10,1... | collective-permute-start | bytes 17576 | tf_op jit(solution)/shard_map/ppermute | solution.py:217
  28.2 1.0 %copy-start.4 = (bf16[256,1536]{1,0:T(8,128)(2,1)}, bf16[256,1536]{1,0:T(8,128)(2,1)S(1)}, u32[]{:S(2)}) copy-start(bf16[256,1536]{1,0:T(8,128)(2,1)S(1)} %shard_map.87.loc_hbm) | copy-start | bytes 2359300
  29.7 6.1 %copy-start.1 = (bf16[36,488,488]{2,1,0:T(8,128)(2,1)S(1)}, bf16[36,488,488]{2,1,0:T(8,128)(2,1)}, u32[]{:S(2)}) copy-start(bf16[36,488,488]{2,1,0:T(8,128)(2,1)} %t_ref) | copy-start | bytes 51439108
  42.2 6.5 %copy-start = (bf16[36,512,512]{2,1,0:T(8,128)(2,1)}, bf16[36,512,512]{2,1,0:T(8,128)(2,1)S(1)}, u32[]{:S(2)}) copy-start(bf16[36,512,512]{2,1,0:T(8,128)(2,1)S(1)} %shard_map.88.t_hbm) | copy-start | bytes 56623108

commit v3 on v2

--- a/solution.py
+++ b/solution.py
@@ -31,16 +31,17 @@
     channels, points, slots = multipoles.shape
     ghosts = send_slots.shape[1]
     half = slots // 2
+    block = 256
     return pl.pallas_call(
         pack_kernel,
-        grid=(1,),
+        grid=(ghosts // block,),
         in_specs=[
             pl.BlockSpec((channels, points, half), lambda i: (0, 0, 0)),
-            pl.BlockSpec((1, ghosts), lambda i: (0, 0)),
+            pl.BlockSpec((1, block), lambda i: (0, i)),
         ],
-        out_specs=pl.BlockSpec((ghosts, channels * KPAD), lambda i: (0, 0)),
+        out_specs=pl.BlockSpec((block, channels * KPAD), lambda i: (i, 0)),
         out_shape=jax.ShapeDtypeStruct((ghosts, channels * KPAD), BF16),
-        compiler_params=pltpu.CompilerParams(vmem_limit_bytes=40 * 2**20),
+        compiler_params=pltpu.CompilerParams(vmem_limit_bytes=60 * 2**20),
     )(multipoles, send_slots)
 
 
@@ -87,13 +88,13 @@
 
 
 def m2l_kernel(
-    vl_ref, live_ref, arr_hbm, loc_hbm, t_hbm, out_ref, buf, acc, arr_ref, loc_ref, t_ref, loc_sem, arr_sem, t_sem, *, depth, batch
+    vl_ref, live_ref, arr_hbm, loc_hbm, t_hbm, out_hbm, buf, acc, arr_ref, loc_ref, t_ref, stage, loc_sem, arr_sem, t_sem, out_sem, *, depth, batch
 ):
     slots = loc_ref.shape[0]
     ghosts = arr_ref.shape[0]
     parts = arr_sem.shape[0]
     span = ghosts // parts
-    channels, points, _ = out_ref.shape
+    channels, points, _ = stage.shape
     chunks = KPAD // LANES
     groups = t_hbm.shape[0] // depth
     laps = groups // 2
@@ -135,13 +136,13 @@
     for k in range(parts):
         part_copy(k).start()
     ops_copy(0).start()
+    acc[...] = jnp.zeros_like(acc)
     loc_copy.wait()
     fill(loc_ref, 0, slots, 0)
     for k in range(parts):
         part_copy(k).wait()
         fill(arr_ref, k * span, span, slots + k * span)
     buf[pl.ds((slots + ghosts) * BOX, 16), :] = jnp.zeros((16, LANES), F32)
-    acc[...] = jnp.zeros_like(acc)
     for p in range(depth):
         gather(p, p, 0, slots)
 
@@ -179,8 +180,13 @@
 
     lax.fori_loop(0, laps, lap, 0)
     keep = lax.broadcasted_iota(jnp.int32, (1, slots), 1) < live_ref[0]
+    out_copies = []
     for c in range(channels):
-        out_ref[c] = jnp.where(keep, acc[c].T[:points], 0.0)
+        stage[c] = jnp.where(keep, acc[c].T[:points], 0.0)
+        out_copies.append(pltpu.make_async_copy(stage.at[c], out_hbm.at[c], out_sem.at[c]))
+        out_copies[c].start()
+    for copy in out_copies:
+        copy.wait()
 
 
 def m2l(cols, live, arrived, local, ops, channels, points):
@@ -190,18 +196,20 @@
     smem = pl.BlockSpec(memory_space=pltpu.SMEM)
     hbm = pl.BlockSpec(memory_space=pl.ANY)
     return pl.pallas_call(
-        functools.partial(m2l_kernel, depth=depth, batch=16),
+        functools.partial(m2l_kernel, depth=depth, batch=8),
         in_specs=[smem, smem, hbm, hbm, hbm],
-        out_specs=pl.BlockSpec(memory_space=pltpu.VMEM),
+        out_specs=hbm,
         scratch_shapes=[
             pltpu.VMEM(((slots + ghosts + 4 + 2 * depth * slots) * BOX, LANES), F32),
             pltpu.VMEM((channels, slots, KPAD), F32),
             pltpu.VMEM(arrived.shape, BF16),
             pltpu.VMEM(local.shape, BF16),
             pltpu.VMEM((2, 2 * depth, KPAD, KPAD), BF16),
+            pltpu.VMEM((channels, points, slots), F32),
             pltpu.SemaphoreType.DMA,
             pltpu.SemaphoreType.DMA((4,)),
             pltpu.SemaphoreType.DMA((2,)),
+            pltpu.SemaphoreType.DMA((channels,)),
         ],
         out_shape=jax.ShapeDtypeStruct((channels, points, slots), F32),
         compiler_params=pltpu.CompilerParams(vmem_limit_bytes=56 * 2**20),

time: 87.7 us -> 86.3 us (0.984)
  local copies, waits for them, and re-layouts: 16.8 us -> 15 us
    unnamed x18 -> x14, local copies, waits for them, and re-layouts: 15.3 us -> 13.5 us
where the time goes in v3:
time: 86.3 us; the launch traced here: 85.9 us
  Pallas kernels  38.5 us (45%)
  starting transfers between devices  17.5 us (20%)
  local copies, waits for them, and re-layouts  15 us (17%)
  waiting for transfers between devices  7.84 us (9%)
  matrix products  3.38 us (4%)
  other arithmetic  2.22 us (3%)
  between operations  1.5 us (2%)
    pallas_call x1, Pallas kernels, m2l(): pl.pallas_call(functools.partial(m2l_kernel, depth=depth, batch=8), in_sp...  27.5 us
    unnamed x14, local copies, waits for them, and re-layouts  13.5 us
    all_to_all x1, starting transfers between devices, body(): lax.all_to_all(outgoing.reshape(dev_count, ghosts // dev_count, width), '...  11.9 us
    pallas_call x1, Pallas kernels, padded_ops(): pl.pallas_call(ops_kernel, grid=(rel // count,), in_specs=[pl.BlockSpec((...  6.32 us
    ppermute x2, starting transfers between devices, shifted(): return lax.ppermute(cells, 'morton', pairs)  5.56 us
    pallas_call x1, Pallas kernels, pack(): pl.pallas_call(pack_kernel, grid=(ghosts // block,), in_specs=[pl.BlockSp...  4.37 us
    all_to_all x1, waiting for transfers between devices, body(): lax.all_to_all(outgoing.reshape(dev_count, ghosts // dev_count, width), '...  3.95 us
    ppermute x2, waiting for transfers between devices, shifted(): return lax.ppermute(cells, 'morton', pairs)  3.89 us
  transfers between devices with their start and end apart: 3, of which 2 were waited for; matrix products, arithmetic and copies ran while one was open for 8% of the time, Pallas kernels for 8%

profile of v3, /device:TPU:1, one launch (start us, length us, event | category | flops | bytes accessed | tf_op | source)
XLA Modules:
  0.0 85.9 jit_solution(3694317813790261059)
XLA Ops:
  0.6 4.4 %shard_map.86 = bf16[1024,1536]{1,0:T(8,128)(2,1)} custom-call(bf16[3,488,256]{2,1,0:T(8,128)(2,1)} %mult_ref.2, s32[1,1024]{1,0:T(1,128)} %slots_ref.1), custom_call_target="tpu_custom_call" | custom-call | tf_op jit(solution)/shard_map/pallas_call | solution.py:35
  5.0 0.0 copy-start.2
  5.0 11.9 %all-to-all-start = ((bf16[128,8,1536]{2,1,0:T(8,128)(2,1)}), bf16[128,8,1536]{2,1,0:T(8,128)(2,1)}, u32[]{:S(2)}, u32[]{:S(2)}) async-start(bf16[128,8,1536]{2,1,0:T(8,128)(2,1)} %bitcast.25), calls=%async_computation | async-start | bytes 6291456 | tf_op jit(solution)/shard_map/all_to_all | solution.py:236
  17.5 0.0 copy-done.2
  17.6 0.3 copy.10
  17.8 0.0 copy-start.5
  17.9 0.0 copy-start.4
  17.9 0.1 select_bitcast_fusion
  18.0 3.4 %fusion = f32[3,32,488,1]{2,1,3,0:T(8,128)S(1)} fusion(bf16[8,488,488]{2,1,0:T(8,128)(2,1)} %param.8, bf16[3,488,32,8]{1,3,2,0:T(8,128)(2,1)S(1)} %select_bitcast_fusion), kind=kOutput, calls=%fused_computation | convolution fusion | flops 365789184 | bytes 4747264 | tf_op jit(solution)/shard_map/oij,cjgo->cig/dot_general | solution.py:248
  21.4 3.0 %collective-permute-start.1 = (f32[3,488]{1,0:T(4,128)S(1)}, f32[3,488]{1,0:T(4,128)S(1)}, u32[]{:S(2)}, u32[]{:S(2)}) collective-permute-start(f32[3,488]{1,0:T(4,128)S(1)} %bitcast.28), channel_id=1, source_target_pairs={{1,0},{2,1},{3,2},{4,3},{5,4},{6,5},{7,6},{8,7},{9,8},{10,9},{11,1... | collective-permute-start | bytes 17576 | tf_op jit(solution)/shard_map/ppermute | solution.py:225
  24.5 2.5 %collective-permute-start = (f32[3,488]{1,0:T(4,128)S(1)}, f32[3,488]{1,0:T(4,128)S(1)}, u32[]{:S(2)}, u32[]{:S(2)}) collective-permute-start(f32[3,488]{1,0:T(4,128)S(1)} %bitcast.29), channel_id=1, source_target_pairs={{0,1},{1,2},{2,3},{3,4},{4,5},{5,6},{6,7},{7,8},{8,9},{9,10},{10,1... | collective-permute-start | bytes 17576 | tf_op jit(solution)/shard_map/ppermute | solution.py:225
  27.1 0.0 copy-done.5
  27.1 0.6 fusion.3
  27.7 0.0 copy-done.4
  27.7 0.3 shard_map.87.loc_hbm
  28.0 0.0 copy-start.3
  28.0 0.9 %copy-done.3 = bf16[256,1536]{1,0:T(8,128)(2,1)} copy-done((bf16[256,1536]{1,0:T(8,128)(2,1)}, bf16[256,1536]{1,0:T(8,128)(2,1)S(1)}, u32[]{:S(2)}) %copy-start.3) | copy-done | bytes 786456
  28.9 0.6 reshape.37.vl_ref
  29.6 0.0 copy-start.1
  29.6 6.1 %copy-done.1 = bf16[36,488,488]{2,1,0:T(8,128)(2,1)S(1)} copy-done((bf16[36,488,488]{2,1,0:T(8,128)(2,1)S(1)}, bf16[36,488,488]{2,1,0:T(8,128)(2,1)}, u32[]{:S(2)}) %copy-start.1) | copy-done | bytes 17146392
  35.7 6.3 %shard_map.88.t_hbm = bf16[36,512,512]{2,1,0:T(8,128)(2,1)S(1)} custom-call(bf16[36,488,488]{2,1,0:T(8,128)(2,1)S(1)} %copy-done.1), custom_call_target="tpu_custom_call" | custom-call | tf_op jit(solution)/shard_map/pallas_call | solution.py:80
  42.0 0.0 copy-start
  42.0 6.5 %copy-done = bf16[36,512,512]{2,1,0:T(8,128)(2,1)} copy-done((bf16[36,512,512]{2,1,0:T(8,128)(2,1)}, bf16[36,512,512]{2,1,0:T(8,128)(2,1)S(1)}, u32[]{:S(2)}) %copy-start) | copy-done | bytes 18874392
  48.5 3.9 %collective-permute-done.1 = f32[3,488]{1,0:T(4,128)S(1)} collective-permute-done((f32[3,488]{1,0:T(4,128)S(1)}, f32[3,488]{1,0:T(4,128)S(1)}, u32[]{:S(2)}, u32[]{:S(2)}) %collective-permute-start.1) | collective-permute-done | bytes 5888 | tf_op jit(solution)/shard_map/ppermute | solution.py:225
  52.4 0.6 broadcast_multiply_fusion
  53.0 0.0 collective-permute-done
  53.0 0.7 broadcast_multiply_fusion.1
  53.7 0.8 select_add_fusion
  54.5 4.0 %all-to-all-done = bf16[128,8,1536]{2,1,0:T(8,128)(2,1)} async-done(((bf16[128,8,1536]{2,1,0:T(8,128)(2,1)}), bf16[128,8,1536]{2,1,0:T(8,128)(2,1)}, u32[]{:S(2)}, u32[]{:S(2)}) %all-to-all-start) | async-done | bytes 3145760 | tf_op jit(solution)/shard_map/all_to_all | solution.py:236
  58.4 27.5 %shard_map.89 = f32[3,488,256]{2,1,0:T(8,128)} custom-call(s32[9216]{0:T(1024)} %reshape.37.vl_ref, s32[1]{0:T(128)} %copy.21.live_ref, bf16[1024,1536]{1,0:T(8,128)(2,1)} %bitcast.2.arr_hbm, bf16[256,1536]{1,0:T(8,128)(2,1)} %copy-done.3, bf16[36,512,512]{2,1,0:T(8,128)(2,1)} %copy-done), custom_call_target="tpu_custom_call" | custom-call | tf_op jit(solution)/shard_map/pallas_call | solution.py:198
  (8 shorter events, 0.0 us)
Async XLA Ops:
  5.0 12.6 %copy-start.2 = (bf16[3,488,256]{2,1,0:T(8,128)(2,1)S(1)}, bf16[3,488,256]{2,1,0:T(8,128)(2,1)}, u32[]{:S(2)}) copy-start(bf16[3,488,256]{2,1,0:T(8,128)(2,1)} %mult_ref.2) | copy-start | bytes 2248708
  5.0 53.4 %all-to-all-start = ((bf16[128,8,1536]{2,1,0:T(8,128)(2,1)}), bf16[128,8,1536]{2,1,0:T(8,128)(2,1)}, u32[]{:S(2)}, u32[]{:S(2)}) async-start(bf16[128,8,1536]{2,1,0:T(8,128)(2,1)} %bitcast.25), calls=%async_computation | async-start | bytes 6291456 | tf_op jit(solution)/shard_map/all_to_all | solution.py:236
  17.8 9.2 %copy-start.5 = (s32[1,2]{1,0:T(1,128)S(1)}, s32[1,2]{1,0:T(1,128)}, u32[]{:S(2)}) copy-start(s32[1,2]{1,0:T(1,128)} %param.11) | copy-start | bytes 28
  17.9 9.8 %copy-start.4 = (s32[256,36]{0,1:T(8,128)S(1)}, s32[256,36]{0,1:T(8,128)}, u32[]{:S(2)}) copy-start(s32[256,36]{0,1:T(8,128)} %param.13) | copy-start | bytes 110596
  21.4 30.9 %collective-permute-start.1 = (f32[3,488]{1,0:T(4,128)S(1)}, f32[3,488]{1,0:T(4,128)S(1)}, u32[]{:S(2)}, u32[]{:S(2)}) collective-permute-start(f32[3,488]{1,0:T(4,128)S(1)} %bitcast.28), channel_id=1, source_target_pairs={{1,0},{2,1},{3,2},{4,3},{5,4},{6,5},{7,6},{8,7},{9,8},{10,9},{11,1... | collective-permute-start | bytes 17576 | tf_op jit(solution)/shard_map/ppermute | solution.py:225
  24.5 28.5 %collective-permute-start = (f32[3,488]{1,0:T(4,128)S(1)}, f32[3,488]{1,0:T(4,128)S(1)}, u32[]{:S(2)}, u32[]{:S(2)}) collective-permute-start(f32[3,488]{1,0:T(4,128)S(1)} %bitcast.29), channel_id=1, source_target_pairs={{0,1},{1,2},{2,3},{3,4},{4,5},{5,6},{6,7},{7,8},{8,9},{9,10},{10,1... | collective-permute-start | bytes 17576 | tf_op jit(solution)/shard_map/ppermute | solution.py:225
  28.0 1.0 %copy-start.3 = (bf16[256,1536]{1,0:T(8,128)(2,1)}, bf16[256,1536]{1,0:T(8,128)(2,1)S(1)}, u32[]{:S(2)}) copy-start(bf16[256,1536]{1,0:T(8,128)(2,1)S(1)} %shard_map.87.loc_hbm) | copy-start | bytes 2359300
  29.6 6.1 %copy-start.1 = (bf16[36,488,488]{2,1,0:T(8,128)(2,1)S(1)}, bf16[36,488,488]{2,1,0:T(8,128)(2,1)}, u32[]{:S(2)}) copy-start(bf16[36,488,488]{2,1,0:T(8,128)(2,1)} %t_ref) | copy-start | bytes 51439108
  42.0 6.5 %copy-start = (bf16[36,512,512]{2,1,0:T(8,128)(2,1)}, bf16[36,512,512]{2,1,0:T(8,128)(2,1)S(1)}, u32[]{:S(2)}) copy-start(bf16[36,512,512]{2,1,0:T(8,128)(2,1)S(1)} %shard_map.88.t_hbm) | copy-start | bytes 56623108

commit v4 on v3

--- a/solution.py
+++ b/solution.py
@@ -14,33 +14,44 @@
 F32 = jnp.float32
 
 
-def pack_kernel(mult_ref, slots_ref, out_ref):
+def pack_kernel(mult_ref, slots_ref, out_hbm, rows_ref, sem):
     channels, points, send_slots = mult_ref.shape
-    ghosts = slots_ref.shape[1]
-    box_ids = lax.broadcasted_iota(jnp.int32, (send_slots, ghosts), 0)
-    onehot = jnp.where(box_ids == slots_ref[...], 1.0, 0.0).astype(BF16)
-    for c in range(channels):
-        rows = lax.dot_general(
-            onehot, mult_ref[c], (((0,), (1,)), ((), ())), preferred_element_type=F32
-        ).astype(BF16)
-        rows = jnp.concatenate([rows, jnp.zeros((ghosts, KPAD - points), BF16)], axis=1)
-        out_ref[:, c * KPAD : (c + 1) * KPAD] = rows
+    parts = sem.shape[0]
+    span = rows_ref.shape[0] // parts
+    box_ids = lax.broadcasted_iota(jnp.int32, (send_slots, span), 0)
+    copies = []
+    for k in range(parts):
+        at = slice(k * span, (k + 1) * span)
+        onehot = jnp.where(box_ids == slots_ref[:, at], 1.0, 0.0).astype(BF16)
+        for c in range(channels):
+            rows = lax.dot_general(
+                onehot, mult_ref[c], (((0,), (1,)), ((), ())), preferred_element_type=F32
+            ).astype(BF16)
+            rows = jnp.concatenate([rows, jnp.zeros((span, KPAD - points), BF16)], axis=1)
+            rows_ref[at, c * KPAD : (c + 1) * KPAD] = rows
+        copies.append(pltpu.make_async_copy(rows_ref.at[at], out_hbm.at[at], sem.at[k]))
+        copies[k].start()
+    for copy in copies:
+        copy.wait()
 
 
 def pack(multipoles, send_slots):
     channels, points, slots = multipoles.shape
     ghosts = send_slots.shape[1]
     half = slots // 2
-    block = 256
     return pl.pallas_call(
         pack_kernel,
-        grid=(ghosts // block,),
+        grid=(1,),
         in_specs=[
             pl.BlockSpec((channels, points, half), lambda i: (0, 0, 0)),
-            pl.BlockSpec((1, block), lambda i: (0, i)),
-        ],
-        out_specs=pl.BlockSpec((block, channels * KPAD), lambda i: (i, 0)),
+            pl.BlockSpec((1, ghosts), lambda i: (0, 0)),
+        ],
+        out_specs=pl.BlockSpec(memory_space=pl.ANY),
         out_shape=jax.ShapeDtypeStruct((ghosts, channels * KPAD), BF16),
+        scratch_shapes=[
+            pltpu.VMEM((ghosts, channels * KPAD), BF16),
+            pltpu.SemaphoreType.DMA((ghosts // 256,)),
+        ],
         compiler_params=pltpu.CompilerParams(vmem_limit_bytes=60 * 2**20),
     )(multipoles, send_slots)
 
@@ -150,11 +161,13 @@
         later = jnp.minimum(s + 1, groups - 1)
         total = depth * slots
         cuts = [total * c // channels // batch * batch for c in range(channels + 1)]
-        for c in range(channels):
+        def fetch(c):
             for p in range(depth):
                 lo, hi = max(cuts[c] - p * slots, 0), min(cuts[c + 1] - p * slots, slots)
                 if lo < hi:
                     gather(later * depth + p, (1 - slot) * depth + p, lo, hi)
+
+        def multiply(c):
             x = jnp.concatenate(
                 [
                     buf[pl.ds(start(slot * depth + p) + c * chunks + q, slots, stride=BOX), :].astype(BF16)
@@ -165,6 +178,10 @@
             )
             w = t_ref[place, slot * depth : (slot + 1) * depth].reshape(depth * KPAD, KPAD)
             acc[c] += jnp.dot(x, w, preferred_element_type=F32)
+
+        for c in range(channels):
+            fetch(c)
+            multiply(c)
 
     def lap(s, carry):
         place = lax.rem(s, 2)

time: 86.3 us -> 85.1 us (0.986)
  Pallas kernels: 38.5 us -> 37.2 us
    pallas_call x1, Pallas kernels: 4.37 us -> 3.08 us  [pack(): pl.pallas_call(pack_kernel, grid=(1,), in_specs=[pl.BlockSpec((channels,...]
where the time goes in v4:
time: 85.1 us; the launch traced here: 84.7 us
  Pallas kernels  37.2 us (44%)
  starting transfers between devices  17.5 us (21%)
  local copies, waits for them, and re-layouts  15 us (18%)
  waiting for transfers between devices  7.84 us (9%)
  matrix products  3.38 us (4%)
  other arithmetic  2.22 us (3%)
  between operations  1.51 us (2%)
    pallas_call x1, Pallas kernels, m2l(): pl.pallas_call(functools.partial(m2l_kernel, depth=depth, batch=8), in_sp...  27.5 us
    unnamed x14, local copies, waits for them, and re-layouts  13.5 us
    all_to_all x1, starting transfers between devices, body(): lax.all_to_all(outgoing.reshape(dev_count, ghosts // dev_count, width), '...  11.9 us
    pallas_call x1, Pallas kernels, padded_ops(): pl.pallas_call(ops_kernel, grid=(rel // count,), in_specs=[pl.BlockSpec((...  6.32 us
    ppermute x2, starting transfers between devices, shifted(): return lax.ppermute(cells, 'morton', pairs)  5.56 us
    all_to_all x1, waiting for transfers between devices, body(): lax.all_to_all(outgoing.reshape(dev_count, ghosts // dev_count, width), '...  3.95 us
    ppermute x2, waiting for transfers between devices, shifted(): return lax.ppermute(cells, 'morton', pairs)  3.89 us
    dot_general x1, matrix products, body(): jnp.einsum('oij,cjgo->cig', upward_ops, children, preferred_element_type=...  3.38 us
  transfers between devices with their start and end apart: 3, of which 2 were waited for; matrix products, arithmetic and copies ran while one was open for 8% of the time, Pallas kernels for 8%

profile of v4, /device:TPU:1, one launch (start us, length us, event | category | flops | bytes accessed | tf_op | source)
XLA Modules:
  0.0 84.7 jit_solution(11256665541768200991)
XLA Ops:
  0.6 3.1 %shard_map.86 = bf16[1024,1536]{1,0:T(8,128)(2,1)} custom-call(bf16[3,488,256]{2,1,0:T(8,128)(2,1)} %mult_ref.2, s32[1,1024]{1,0:T(1,128)} %slots_ref.1), custom_call_target="tpu_custom_call" | custom-call | tf_op jit(solution)/shard_map/pallas_call | solution.py:42
  3.7 0.0 copy-start.2
  3.7 11.9 %all-to-all-start = ((bf16[128,8,1536]{2,1,0:T(8,128)(2,1)}), bf16[128,8,1536]{2,1,0:T(8,128)(2,1)}, u32[]{:S(2)}, u32[]{:S(2)}) async-start(bf16[128,8,1536]{2,1,0:T(8,128)(2,1)} %bitcast.25), calls=%async_computation | async-start | bytes 6291456 | tf_op jit(solution)/shard_map/all_to_all | solution.py:253
  16.3 0.0 copy-done.2
  16.3 0.3 copy.10
  16.6 0.0 copy-start.5
  16.6 0.0 copy-start.4
  16.6 0.1 select_bitcast_fusion
  16.8 3.4 %fusion = f32[3,32,488,1]{2,1,3,0:T(8,128)S(1)} fusion(bf16[8,488,488]{2,1,0:T(8,128)(2,1)} %param.8, bf16[3,488,32,8]{1,3,2,0:T(8,128)(2,1)S(1)} %select_bitcast_fusion), kind=kOutput, calls=%fused_computation | convolution fusion | flops 365789184 | bytes 4747264 | tf_op jit(solution)/shard_map/oij,cjgo->cig/dot_general | solution.py:265
  20.2 3.0 %collective-permute-start.1 = (f32[3,488]{1,0:T(4,128)S(1)}, f32[3,488]{1,0:T(4,128)S(1)}, u32[]{:S(2)}, u32[]{:S(2)}) collective-permute-start(f32[3,488]{1,0:T(4,128)S(1)} %bitcast.28), channel_id=1, source_target_pairs={{1,0},{2,1},{3,2},{4,3},{5,4},{6,5},{7,6},{8,7},{9,8},{10,9},{11,1... | collective-permute-start | bytes 17576 | tf_op jit(solution)/shard_map/ppermute | solution.py:242
  23.3 2.5 %collective-permute-start = (f32[3,488]{1,0:T(4,128)S(1)}, f32[3,488]{1,0:T(4,128)S(1)}, u32[]{:S(2)}, u32[]{:S(2)}) collective-permute-start(f32[3,488]{1,0:T(4,128)S(1)} %bitcast.29), channel_id=1, source_target_pairs={{0,1},{1,2},{2,3},{3,4},{4,5},{5,6},{6,7},{7,8},{8,9},{9,10},{10,1... | collective-permute-start | bytes 17576 | tf_op jit(solution)/shard_map/ppermute | solution.py:242
  25.8 0.0 copy-done.5
  25.8 0.6 fusion.3
  26.4 0.0 copy-done.4
  26.4 0.3 shard_map.87.loc_hbm
  26.7 0.0 copy-start.3
  26.7 0.9 %copy-done.3 = bf16[256,1536]{1,0:T(8,128)(2,1)} copy-done((bf16[256,1536]{1,0:T(8,128)(2,1)}, bf16[256,1536]{1,0:T(8,128)(2,1)S(1)}, u32[]{:S(2)}) %copy-start.3) | copy-done | bytes 786456
  27.7 0.6 reshape.37.vl_ref
  28.3 0.0 copy-start.1
  28.3 6.1 %copy-done.1 = bf16[36,488,488]{2,1,0:T(8,128)(2,1)S(1)} copy-done((bf16[36,488,488]{2,1,0:T(8,128)(2,1)S(1)}, bf16[36,488,488]{2,1,0:T(8,128)(2,1)}, u32[]{:S(2)}) %copy-start.1) | copy-done | bytes 17146392
  34.4 6.3 %shard_map.88.t_hbm = bf16[36,512,512]{2,1,0:T(8,128)(2,1)S(1)} custom-call(bf16[36,488,488]{2,1,0:T(8,128)(2,1)S(1)} %copy-done.1), custom_call_target="tpu_custom_call" | custom-call | tf_op jit(solution)/shard_map/pallas_call | solution.py:91
  40.8 0.0 copy-start
  40.8 6.5 %copy-done = bf16[36,512,512]{2,1,0:T(8,128)(2,1)} copy-done((bf16[36,512,512]{2,1,0:T(8,128)(2,1)}, bf16[36,512,512]{2,1,0:T(8,128)(2,1)S(1)}, u32[]{:S(2)}) %copy-start) | copy-done | bytes 18874392
  47.2 3.9 %collective-permute-done.1 = f32[3,488]{1,0:T(4,128)S(1)} collective-permute-done((f32[3,488]{1,0:T(4,128)S(1)}, f32[3,488]{1,0:T(4,128)S(1)}, u32[]{:S(2)}, u32[]{:S(2)}) %collective-permute-start.1) | collective-permute-done | bytes 5888 | tf_op jit(solution)/shard_map/ppermute | solution.py:242
  51.1 0.6 broadcast_multiply_fusion
  51.8 0.0 collective-permute-done
  51.8 0.7 broadcast_multiply_fusion.1
  52.4 0.8 select_add_fusion
  53.2 4.0 %all-to-all-done = bf16[128,8,1536]{2,1,0:T(8,128)(2,1)} async-done(((bf16[128,8,1536]{2,1,0:T(8,128)(2,1)}), bf16[128,8,1536]{2,1,0:T(8,128)(2,1)}, u32[]{:S(2)}, u32[]{:S(2)}) %all-to-all-start) | async-done | bytes 3145760 | tf_op jit(solution)/shard_map/all_to_all | solution.py:253
  57.2 27.5 %shard_map.89 = f32[3,488,256]{2,1,0:T(8,128)} custom-call(s32[9216]{0:T(1024)} %reshape.37.vl_ref, s32[1]{0:T(128)} %copy.21.live_ref, bf16[1024,1536]{1,0:T(8,128)(2,1)} %bitcast.2.arr_hbm, bf16[256,1536]{1,0:T(8,128)(2,1)} %copy-done.3, bf16[36,512,512]{2,1,0:T(8,128)(2,1)} %copy-done), custom_call_target="tpu_custom_call" | custom-call | tf_op jit(solution)/shard_map/pallas_call | solution.py:215
  (8 shorter events, 0.0 us)
Async XLA Ops:
  3.7 12.6 %copy-start.2 = (bf16[3,488,256]{2,1,0:T(8,128)(2,1)S(1)}, bf16[3,488,256]{2,1,0:T(8,128)(2,1)}, u32[]{:S(2)}) copy-start(bf16[3,488,256]{2,1,0:T(8,128)(2,1)} %mult_ref.2) | copy-start | bytes 2248708
  3.7 53.4 %all-to-all-start = ((bf16[128,8,1536]{2,1,0:T(8,128)(2,1)}), bf16[128,8,1536]{2,1,0:T(8,128)(2,1)}, u32[]{:S(2)}, u32[]{:S(2)}) async-start(bf16[128,8,1536]{2,1,0:T(8,128)(2,1)} %bitcast.25), calls=%async_computation | async-start | bytes 6291456 | tf_op jit(solution)/shard_map/all_to_all | solution.py:253
  16.6 9.2 %copy-start.5 = (s32[1,2]{1,0:T(1,128)S(1)}, s32[1,2]{1,0:T(1,128)}, u32[]{:S(2)}) copy-start(s32[1,2]{1,0:T(1,128)} %param.11) | copy-start | bytes 28
  16.6 9.8 %copy-start.4 = (s32[256,36]{0,1:T(8,128)S(1)}, s32[256,36]{0,1:T(8,128)}, u32[]{:S(2)}) copy-start(s32[256,36]{0,1:T(8,128)} %param.13) | copy-start | bytes 110596
  20.2 30.9 %collective-permute-start.1 = (f32[3,488]{1,0:T(4,128)S(1)}, f32[3,488]{1,0:T(4,128)S(1)}, u32[]{:S(2)}, u32[]{:S(2)}) collective-permute-start(f32[3,488]{1,0:T(4,128)S(1)} %bitcast.28), channel_id=1, source_target_pairs={{1,0},{2,1},{3,2},{4,3},{5,4},{6,5},{7,6},{8,7},{9,8},{10,9},{11,1... | collective-permute-start | bytes 17576 | tf_op jit(solution)/shard_map/ppermute | solution.py:242
  23.3 28.5 %collective-permute-start = (f32[3,488]{1,0:T(4,128)S(1)}, f32[3,488]{1,0:T(4,128)S(1)}, u32[]{:S(2)}, u32[]{:S(2)}) collective-permute-start(f32[3,488]{1,0:T(4,128)S(1)} %bitcast.29), channel_id=1, source_target_pairs={{0,1},{1,2},{2,3},{3,4},{4,5},{5,6},{6,7},{7,8},{8,9},{9,10},{10,1... | collective-permute-start | bytes 17576 | tf_op jit(solution)/shard_map/ppermute | solution.py:242
  26.7 1.0 %copy-start.3 = (bf16[256,1536]{1,0:T(8,128)(2,1)}, bf16[256,1536]{1,0:T(8,128)(2,1)S(1)}, u32[]{:S(2)}) copy-start(bf16[256,1536]{1,0:T(8,128)(2,1)S(1)} %shard_map.87.loc_hbm) | copy-start | bytes 2359300
  28.3 6.1 %copy-start.1 = (bf16[36,488,488]{2,1,0:T(8,128)(2,1)S(1)}, bf16[36,488,488]{2,1,0:T(8,128)(2,1)}, u32[]{:S(2)}) copy-start(bf16[36,488,488]{2,1,0:T(8,128)(2,1)} %t_ref) | copy-start | bytes 51439108
  40.8 6.5 %copy-start = (bf16[36,512,512]{2,1,0:T(8,128)(2,1)}, bf16[36,512,512]{2,1,0:T(8,128)(2,1)S(1)}, u32[]{:S(2)}) copy-start(bf16[36,512,512]{2,1,0:T(8,128)(2,1)S(1)} %shard_map.88.t_hbm) | copy-start | bytes 56623108

commit v5 on v4

--- a/solution.py
+++ b/solution.py
@@ -157,7 +157,7 @@
     for p in range(depth):
         gather(p, p, 0, slots)
 
-    def group(s, slot, place):
+    def group(s, slot, place, last=False):
         later = jnp.minimum(s + 1, groups - 1)
         total = depth * slots
         cuts = [total * c // channels // batch * batch for c in range(channels + 1)]
@@ -180,30 +180,36 @@
             acc[c] += jnp.dot(x, w, preferred_element_type=F32)
 
         for c in range(channels):
-            fetch(c)
+            if not last:
+                fetch(c)
             multiply(c)
+            if last:
+                finish(c)
+
+    keep = lax.broadcasted_iota(jnp.int32, (1, slots), 1) < live_ref[0]
+
+    def out_copy(c):
+        return pltpu.make_async_copy(stage.at[c], out_hbm.at[c], out_sem.at[c])
+
+    def finish(c):
+        stage[c] = jnp.where(keep, acc[c].T[:points], 0.0)
+        out_copy(c).start()
 
     def lap(s, carry):
         place = lax.rem(s, 2)
         ops_copy(s).wait()
-
-        @pl.when(s + 1 < laps)
-        def _():
-            ops_copy(s + 1).start()
-
+        ops_copy(s + 1).start()
         group(2 * s, 0, place)
         group(2 * s + 1, 1, place)
         return carry
 
-    lax.fori_loop(0, laps, lap, 0)
-    keep = lax.broadcasted_iota(jnp.int32, (1, slots), 1) < live_ref[0]
-    out_copies = []
+    lax.fori_loop(0, laps - 1, lap, 0)
+    end = laps - 1
+    ops_copy(end).wait()
+    group(2 * end, 0, end % 2)
+    group(2 * end + 1, 1, end % 2, last=True)
     for c in range(channels):
-        stage[c] = jnp.where(keep, acc[c].T[:points], 0.0)
-        out_copies.append(pltpu.make_async_copy(stage.at[c], out_hbm.at[c], out_sem.at[c]))
-        out_copies[c].start()
-    for copy in out_copies:
-        copy.wait()
+        out_copy(c).wait()
 
 
 def m2l(cols, live, arrived, local, ops, channels, points):

time: 85.1 us -> 84.4 us (level)
  no operation moved by 1% of the time
where the time goes in v5:
time: 84.4 us; the launch traced here: 84 us
  Pallas kernels  36.6 us (43%)
  starting transfers between devices  17.5 us (21%)
  local copies, waits for them, and re-layouts  15 us (18%)
  waiting for transfers between devices  7.84 us (9%)
  matrix products  3.38 us (4%)
  other arithmetic  2.22 us (3%)
  between operations  1.51 us (2%)
    pallas_call x1, Pallas kernels, m2l(): pl.pallas_call(functools.partial(m2l_kernel, depth=depth, batch=8), in_sp...  26.9 us
    unnamed x14, local copies, waits for them, and re-layouts  13.5 us
    all_to_all x1, starting transfers between devices, body(): lax.all_to_all(outgoing.reshape(dev_count, ghosts // dev_count, width), '...  11.9 us
    pallas_call x1, Pallas kernels, padded_ops(): pl.pallas_call(ops_kernel, grid=(rel // count,), in_specs=[pl.BlockSpec((...  6.32 us
    ppermute x2, starting transfers between devices, shifted(): return lax.ppermute(cells, 'morton', pairs)  5.56 us
    all_to_all x1, waiting for transfers between devices, body(): lax.all_to_all(outgoing.reshape(dev_count, ghosts // dev_count, width), '...  3.95 us
    ppermute x2, waiting for transfers between devices, shifted(): return lax.ppermute(cells, 'morton', pairs)  3.89 us
    dot_general x1, matrix products, body(): jnp.einsum('oij,cjgo->cig', upward_ops, children, preferred_element_type=...  3.38 us
  transfers between devices with their start and end apart: 3, of which 2 were waited for; matrix products, arithmetic and copies ran while one was open for 8% of the time, Pallas kernels for 8%

profile of v5, /device:TPU:1, one launch (start us, length us, event | category | flops | bytes accessed | tf_op | source)
XLA Modules:
  0.0 84.0 jit_solution(4261980241173300560)
XLA Ops:
  0.6 3.1 %shard_map.86 = bf16[1024,1536]{1,0:T(8,128)(2,1)} custom-call(bf16[3,488,256]{2,1,0:T(8,128)(2,1)} %mult_ref.2, s32[1,1024]{1,0:T(1,128)} %slots_ref.1), custom_call_target="tpu_custom_call" | custom-call | tf_op jit(solution)/shard_map/pallas_call | solution.py:42
  3.7 0.0 copy-start.2
  3.7 11.9 %all-to-all-start = ((bf16[128,8,1536]{2,1,0:T(8,128)(2,1)}), bf16[128,8,1536]{2,1,0:T(8,128)(2,1)}, u32[]{:S(2)}, u32[]{:S(2)}) async-start(bf16[128,8,1536]{2,1,0:T(8,128)(2,1)} %bitcast.25), calls=%async_computation | async-start | bytes 6291456 | tf_op jit(solution)/shard_map/all_to_all | solution.py:259
  16.3 0.0 copy-done.2
  16.3 0.3 copy.10
  16.6 0.0 copy-start.5
  16.6 0.0 copy-start.4
  16.6 0.1 select_bitcast_fusion
  16.8 3.4 %fusion = f32[3,32,488,1]{2,1,3,0:T(8,128)S(1)} fusion(bf16[8,488,488]{2,1,0:T(8,128)(2,1)} %param.8, bf16[3,488,32,8]{1,3,2,0:T(8,128)(2,1)S(1)} %select_bitcast_fusion), kind=kOutput, calls=%fused_computation | convolution fusion | flops 365789184 | bytes 4747264 | tf_op jit(solution)/shard_map/oij,cjgo->cig/dot_general | solution.py:271
  20.2 3.0 %collective-permute-start.1 = (f32[3,488]{1,0:T(4,128)S(1)}, f32[3,488]{1,0:T(4,128)S(1)}, u32[]{:S(2)}, u32[]{:S(2)}) collective-permute-start(f32[3,488]{1,0:T(4,128)S(1)} %bitcast.28), channel_id=1, source_target_pairs={{1,0},{2,1},{3,2},{4,3},{5,4},{6,5},{7,6},{8,7},{9,8},{10,9},{11,1... | collective-permute-start | bytes 17576 | tf_op jit(solution)/shard_map/ppermute | solution.py:248
  23.3 2.5 %collective-permute-start = (f32[3,488]{1,0:T(4,128)S(1)}, f32[3,488]{1,0:T(4,128)S(1)}, u32[]{:S(2)}, u32[]{:S(2)}) collective-permute-start(f32[3,488]{1,0:T(4,128)S(1)} %bitcast.29), channel_id=1, source_target_pairs={{0,1},{1,2},{2,3},{3,4},{4,5},{5,6},{6,7},{7,8},{8,9},{9,10},{10,1... | collective-permute-start | bytes 17576 | tf_op jit(solution)/shard_map/ppermute | solution.py:248
  25.8 0.0 copy-done.5
  25.8 0.6 fusion.3
  26.4 0.0 copy-done.4
  26.4 0.3 shard_map.87.loc_hbm
  26.7 0.0 copy-start.3
  26.7 0.9 %copy-done.3 = bf16[256,1536]{1,0:T(8,128)(2,1)} copy-done((bf16[256,1536]{1,0:T(8,128)(2,1)}, bf16[256,1536]{1,0:T(8,128)(2,1)S(1)}, u32[]{:S(2)}) %copy-start.3) | copy-done | bytes 786456
  27.7 0.6 reshape.37.vl_ref
  28.3 0.0 copy-start.1
  28.3 6.1 %copy-done.1 = bf16[36,488,488]{2,1,0:T(8,128)(2,1)S(1)} copy-done((bf16[36,488,488]{2,1,0:T(8,128)(2,1)S(1)}, bf16[36,488,488]{2,1,0:T(8,128)(2,1)}, u32[]{:S(2)}) %copy-start.1) | copy-done | bytes 17146392
  34.4 6.3 %shard_map.88.t_hbm = bf16[36,512,512]{2,1,0:T(8,128)(2,1)S(1)} custom-call(bf16[36,488,488]{2,1,0:T(8,128)(2,1)S(1)} %copy-done.1), custom_call_target="tpu_custom_call" | custom-call | tf_op jit(solution)/shard_map/pallas_call | solution.py:91
  40.8 0.0 copy-start
  40.8 6.5 %copy-done = bf16[36,512,512]{2,1,0:T(8,128)(2,1)} copy-done((bf16[36,512,512]{2,1,0:T(8,128)(2,1)}, bf16[36,512,512]{2,1,0:T(8,128)(2,1)S(1)}, u32[]{:S(2)}) %copy-start) | copy-done | bytes 18874392
  47.2 3.9 %collective-permute-done.1 = f32[3,488]{1,0:T(4,128)S(1)} collective-permute-done((f32[3,488]{1,0:T(4,128)S(1)}, f32[3,488]{1,0:T(4,128)S(1)}, u32[]{:S(2)}, u32[]{:S(2)}) %collective-permute-start.1) | collective-permute-done | bytes 5888 | tf_op jit(solution)/shard_map/ppermute | solution.py:248
  51.1 0.6 broadcast_multiply_fusion
  51.8 0.0 collective-permute-done
  51.8 0.7 broadcast_multiply_fusion.1
  52.4 0.8 select_add_fusion
  53.2 4.0 %all-to-all-done = bf16[128,8,1536]{2,1,0:T(8,128)(2,1)} async-done(((bf16[128,8,1536]{2,1,0:T(8,128)(2,1)}), bf16[128,8,1536]{2,1,0:T(8,128)(2,1)}, u32[]{:S(2)}, u32[]{:S(2)}) %all-to-all-start) | async-done | bytes 3145760 | tf_op jit(solution)/shard_map/all_to_all | solution.py:259
  57.2 26.9 %shard_map.89 = f32[3,488,256]{2,1,0:T(8,128)} custom-call(s32[9216]{0:T(1024)} %reshape.37.vl_ref, s32[1]{0:T(128)} %copy.21.live_ref, bf16[1024,1536]{1,0:T(8,128)(2,1)} %bitcast.2.arr_hbm, bf16[256,1536]{1,0:T(8,128)(2,1)} %copy-done.3, bf16[36,512,512]{2,1,0:T(8,128)(2,1)} %copy-done), custom_call_target="tpu_custom_call" | custom-call | tf_op jit(solution)/shard_map/pallas_call | solution.py:221
  (8 shorter events, 0.0 us)
Async XLA Ops:
  3.7 12.6 %copy-start.2 = (bf16[3,488,256]{2,1,0:T(8,128)(2,1)S(1)}, bf16[3,488,256]{2,1,0:T(8,128)(2,1)}, u32[]{:S(2)}) copy-start(bf16[3,488,256]{2,1,0:T(8,128)(2,1)} %mult_ref.2) | copy-start | bytes 2248708
  3.7 53.4 %all-to-all-start = ((bf16[128,8,1536]{2,1,0:T(8,128)(2,1)}), bf16[128,8,1536]{2,1,0:T(8,128)(2,1)}, u32[]{:S(2)}, u32[]{:S(2)}) async-start(bf16[128,8,1536]{2,1,0:T(8,128)(2,1)} %bitcast.25), calls=%async_computation | async-start | bytes 6291456 | tf_op jit(solution)/shard_map/all_to_all | solution.py:259
  16.6 9.2 %copy-start.5 = (s32[1,2]{1,0:T(1,128)S(1)}, s32[1,2]{1,0:T(1,128)}, u32[]{:S(2)}) copy-start(s32[1,2]{1,0:T(1,128)} %param.11) | copy-start | bytes 28
  16.6 9.8 %copy-start.4 = (s32[256,36]{0,1:T(8,128)S(1)}, s32[256,36]{0,1:T(8,128)}, u32[]{:S(2)}) copy-start(s32[256,36]{0,1:T(8,128)} %param.13) | copy-start | bytes 110596
  20.2 30.9 %collective-permute-start.1 = (f32[3,488]{1,0:T(4,128)S(1)}, f32[3,488]{1,0:T(4,128)S(1)}, u32[]{:S(2)}, u32[]{:S(2)}) collective-permute-start(f32[3,488]{1,0:T(4,128)S(1)} %bitcast.28), channel_id=1, source_target_pairs={{1,0},{2,1},{3,2},{4,3},{5,4},{6,5},{7,6},{8,7},{9,8},{10,9},{11,1... | collective-permute-start | bytes 17576 | tf_op jit(solution)/shard_map/ppermute | solution.py:248
  23.3 28.5 %collective-permute-start = (f32[3,488]{1,0:T(4,128)S(1)}, f32[3,488]{1,0:T(4,128)S(1)}, u32[]{:S(2)}, u32[]{:S(2)}) collective-permute-start(f32[3,488]{1,0:T(4,128)S(1)} %bitcast.29), channel_id=1, source_target_pairs={{0,1},{1,2},{2,3},{3,4},{4,5},{5,6},{6,7},{7,8},{8,9},{9,10},{10,1... | collective-permute-start | bytes 17576 | tf_op jit(solution)/shard_map/ppermute | solution.py:248
  26.7 1.0 %copy-start.3 = (bf16[256,1536]{1,0:T(8,128)(2,1)}, bf16[256,1536]{1,0:T(8,128)(2,1)S(1)}, u32[]{:S(2)}) copy-start(bf16[256,1536]{1,0:T(8,128)(2,1)S(1)} %shard_map.87.loc_hbm) | copy-start | bytes 2359300
  28.3 6.1 %copy-start.1 = (bf16[36,488,488]{2,1,0:T(8,128)(2,1)S(1)}, bf16[36,488,488]{2,1,0:T(8,128)(2,1)}, u32[]{:S(2)}) copy-start(bf16[36,488,488]{2,1,0:T(8,128)(2,1)} %t_ref) | copy-start | bytes 51439108
  40.8 6.5 %copy-start = (bf16[36,512,512]{2,1,0:T(8,128)(2,1)}, bf16[36,512,512]{2,1,0:T(8,128)(2,1)S(1)}, u32[]{:S(2)}) copy-start(bf16[36,512,512]{2,1,0:T(8,128)(2,1)S(1)} %shard_map.88.t_hbm) | copy-start | bytes 56623108

commit v6 on v5

--- a/solution.py
+++ b/solution.py
@@ -215,7 +215,7 @@
 def m2l(cols, live, arrived, local, ops, channels, points):
     ghosts = arrived.shape[0]
     slots = local.shape[0]
-    depth = 2
+    depth = 3
     smem = pl.BlockSpec(memory_space=pltpu.SMEM)
     hbm = pl.BlockSpec(memory_space=pl.ANY)
     return pl.pallas_call(

time: 84.4 us -> 84.5 us (level)
  no operation moved by 1% of the time
where the time goes in v6:
time: 84.5 us; the launch traced here: 84.1 us
  Pallas kernels  36.6 us (43%)
  starting transfers between devices  17.5 us (21%)
  local copies, waits for them, and re-layouts  15 us (18%)
  waiting for transfers between devices  7.84 us (9%)
  matrix products  3.38 us (4%)
  other arithmetic  2.22 us (3%)
  between operations  1.51 us (2%)
    pallas_call x1, Pallas kernels, m2l(): pl.pallas_call(functools.partial(m2l_kernel, depth=depth, batch=8), in_sp...  26.9 us
    unnamed x14, local copies, waits for them, and re-layouts  13.5 us
    all_to_all x1, starting transfers between devices, body(): lax.all_to_all(outgoing.reshape(dev_count, ghosts // dev_count, width), '...  11.9 us
    pallas_call x1, Pallas kernels, padded_ops(): pl.pallas_call(ops_kernel, grid=(rel // count,), in_specs=[pl.BlockSpec((...  6.32 us
    ppermute x2, starting transfers between devices, shifted(): return lax.ppermute(cells, 'morton', pairs)  5.56 us
    all_to_all x1, waiting for transfers between devices, body(): lax.all_to_all(outgoing.reshape(dev_count, ghosts // dev_count, width), '...  3.95 us
    ppermute x2, waiting for transfers between devices, shifted(): return lax.ppermute(cells, 'morton', pairs)  3.89 us
    dot_general x1, matrix products, body(): jnp.einsum('oij,cjgo->cig', upward_ops, children, preferred_element_type=...  3.38 us
  transfers between devices with their start and end apart: 3, of which 2 were waited for; matrix products, arithmetic and copies ran while one was open for 8% of the time, Pallas kernels for 8%

profile of v6, /device:TPU:1, one launch (start us, length us, event | category | flops | bytes accessed | tf_op | source)
XLA Modules:
  0.0 84.1 jit_solution(5134314935873088195)
XLA Ops:
  0.6 3.1 %shard_map.86 = bf16[1024,1536]{1,0:T(8,128)(2,1)} custom-call(bf16[3,488,256]{2,1,0:T(8,128)(2,1)} %mult_ref.2, s32[1,1024]{1,0:T(1,128)} %slots_ref.1), custom_call_target="tpu_custom_call" | custom-call | tf_op jit(solution)/shard_map/pallas_call | solution.py:42
  3.7 0.0 copy-start.2
  3.7 11.9 %all-to-all-start = ((bf16[128,8,1536]{2,1,0:T(8,128)(2,1)}), bf16[128,8,1536]{2,1,0:T(8,128)(2,1)}, u32[]{:S(2)}, u32[]{:S(2)}) async-start(bf16[128,8,1536]{2,1,0:T(8,128)(2,1)} %bitcast.25), calls=%async_computation | async-start | bytes 6291456 | tf_op jit(solution)/shard_map/all_to_all | solution.py:259
  16.3 0.0 copy-done.2
  16.3 0.3 copy.10
  16.6 0.0 copy-start.5
  16.6 0.0 copy-start.4
  16.6 0.1 select_bitcast_fusion
  16.8 3.4 %fusion = f32[3,32,488,1]{2,1,3,0:T(8,128)S(1)} fusion(bf16[8,488,488]{2,1,0:T(8,128)(2,1)} %param.8, bf16[3,488,32,8]{1,3,2,0:T(8,128)(2,1)S(1)} %select_bitcast_fusion), kind=kOutput, calls=%fused_computation | convolution fusion | flops 365789184 | bytes 4747264 | tf_op jit(solution)/shard_map/oij,cjgo->cig/dot_general | solution.py:271
  20.2 3.0 %collective-permute-start.1 = (f32[3,488]{1,0:T(4,128)S(1)}, f32[3,488]{1,0:T(4,128)S(1)}, u32[]{:S(2)}, u32[]{:S(2)}) collective-permute-start(f32[3,488]{1,0:T(4,128)S(1)} %bitcast.28), channel_id=1, source_target_pairs={{1,0},{2,1},{3,2},{4,3},{5,4},{6,5},{7,6},{8,7},{9,8},{10,9},{11,1... | collective-permute-start | bytes 17576 | tf_op jit(solution)/shard_map/ppermute | solution.py:248
  23.3 2.5 %collective-permute-start = (f32[3,488]{1,0:T(4,128)S(1)}, f32[3,488]{1,0:T(4,128)S(1)}, u32[]{:S(2)}, u32[]{:S(2)}) collective-permute-start(f32[3,488]{1,0:T(4,128)S(1)} %bitcast.29), channel_id=1, source_target_pairs={{0,1},{1,2},{2,3},{3,4},{4,5},{5,6},{6,7},{7,8},{8,9},{9,10},{10,1... | collective-permute-start | bytes 17576 | tf_op jit(solution)/shard_map/ppermute | solution.py:248
  25.8 0.0 copy-done.5
  25.8 0.6 fusion.3
  26.4 0.0 copy-done.4
  26.4 0.3 shard_map.87.loc_hbm
  26.7 0.0 copy-start.3
  26.7 0.9 %copy-done.3 = bf16[256,1536]{1,0:T(8,128)(2,1)} copy-done((bf16[256,1536]{1,0:T(8,128)(2,1)}, bf16[256,1536]{1,0:T(8,128)(2,1)S(1)}, u32[]{:S(2)}) %copy-start.3) | copy-done | bytes 786456
  27.7 0.6 reshape.37.vl_ref
  28.3 0.0 copy-start.1
  28.3 6.1 %copy-done.1 = bf16[36,488,488]{2,1,0:T(8,128)(2,1)S(1)} copy-done((bf16[36,488,488]{2,1,0:T(8,128)(2,1)S(1)}, bf16[36,488,488]{2,1,0:T(8,128)(2,1)}, u32[]{:S(2)}) %copy-start.1) | copy-done | bytes 17146392
  34.4 6.3 %shard_map.88.t_hbm = bf16[36,512,512]{2,1,0:T(8,128)(2,1)S(1)} custom-call(bf16[36,488,488]{2,1,0:T(8,128)(2,1)S(1)} %copy-done.1), custom_call_target="tpu_custom_call" | custom-call | tf_op jit(solution)/shard_map/pallas_call | solution.py:91
  40.8 0.0 copy-start
  40.8 6.5 %copy-done = bf16[36,512,512]{2,1,0:T(8,128)(2,1)} copy-done((bf16[36,512,512]{2,1,0:T(8,128)(2,1)}, bf16[36,512,512]{2,1,0:T(8,128)(2,1)S(1)}, u32[]{:S(2)}) %copy-start) | copy-done | bytes 18874392
  47.2 3.9 %collective-permute-done.1 = f32[3,488]{1,0:T(4,128)S(1)} collective-permute-done((f32[3,488]{1,0:T(4,128)S(1)}, f32[3,488]{1,0:T(4,128)S(1)}, u32[]{:S(2)}, u32[]{:S(2)}) %collective-permute-start.1) | collective-permute-done | bytes 5888 | tf_op jit(solution)/shard_map/ppermute | solution.py:248
  51.1 0.6 broadcast_multiply_fusion
  51.8 0.0 collective-permute-done
  51.8 0.7 broadcast_multiply_fusion.1
  52.4 0.8 select_add_fusion
  53.2 4.0 %all-to-all-done = bf16[128,8,1536]{2,1,0:T(8,128)(2,1)} async-done(((bf16[128,8,1536]{2,1,0:T(8,128)(2,1)}), bf16[128,8,1536]{2,1,0:T(8,128)(2,1)}, u32[]{:S(2)}, u32[]{:S(2)}) %all-to-all-start) | async-done | bytes 3145760 | tf_op jit(solution)/shard_map/all_to_all | solution.py:259
  57.2 26.9 %shard_map.89 = f32[3,488,256]{2,1,0:T(8,128)} custom-call(s32[9216]{0:T(1024)} %reshape.37.vl_ref, s32[1]{0:T(128)} %copy.21.live_ref, bf16[1024,1536]{1,0:T(8,128)(2,1)} %bitcast.2.arr_hbm, bf16[256,1536]{1,0:T(8,128)(2,1)} %copy-done.3, bf16[36,512,512]{2,1,0:T(8,128)(2,1)} %copy-done), custom_call_target="tpu_custom_call" | custom-call | tf_op jit(solution)/shard_map/pallas_call | solution.py:221
  (8 shorter events, 0.0 us)
Async XLA Ops:
  3.7 12.6 %copy-start.2 = (bf16[3,488,256]{2,1,0:T(8,128)(2,1)S(1)}, bf16[3,488,256]{2,1,0:T(8,128)(2,1)}, u32[]{:S(2)}) copy-start(bf16[3,488,256]{2,1,0:T(8,128)(2,1)} %mult_ref.2) | copy-start | bytes 2248708
  3.7 53.4 %all-to-all-start = ((bf16[128,8,1536]{2,1,0:T(8,128)(2,1)}), bf16[128,8,1536]{2,1,0:T(8,128)(2,1)}, u32[]{:S(2)}, u32[]{:S(2)}) async-start(bf16[128,8,1536]{2,1,0:T(8,128)(2,1)} %bitcast.25), calls=%async_computation | async-start | bytes 6291456 | tf_op jit(solution)/shard_map/all_to_all | solution.py:259
  16.6 9.2 %copy-start.5 = (s32[1,2]{1,0:T(1,128)S(1)}, s32[1,2]{1,0:T(1,128)}, u32[]{:S(2)}) copy-start(s32[1,2]{1,0:T(1,128)} %param.11) | copy-start | bytes 28
  16.6 9.8 %copy-start.4 = (s32[256,36]{0,1:T(8,128)S(1)}, s32[256,36]{0,1:T(8,128)}, u32[]{:S(2)}) copy-start(s32[256,36]{0,1:T(8,128)} %param.13) | copy-start | bytes 110596
  20.2 30.9 %collective-permute-start.1 = (f32[3,488]{1,0:T(4,128)S(1)}, f32[3,488]{1,0:T(4,128)S(1)}, u32[]{:S(2)}, u32[]{:S(2)}) collective-permute-start(f32[3,488]{1,0:T(4,128)S(1)} %bitcast.28), channel_id=1, source_target_pairs={{1,0},{2,1},{3,2},{4,3},{5,4},{6,5},{7,6},{8,7},{9,8},{10,9},{11,1... | collective-permute-start | bytes 17576 | tf_op jit(solution)/shard_map/ppermute | solution.py:248
  23.3 28.5 %collective-permute-start = (f32[3,488]{1,0:T(4,128)S(1)}, f32[3,488]{1,0:T(4,128)S(1)}, u32[]{:S(2)}, u32[]{:S(2)}) collective-permute-start(f32[3,488]{1,0:T(4,128)S(1)} %bitcast.29), channel_id=1, source_target_pairs={{0,1},{1,2},{2,3},{3,4},{4,5},{5,6},{6,7},{7,8},{8,9},{9,10},{10,1... | collective-permute-start | bytes 17576 | tf_op jit(solution)/shard_map/ppermute | solution.py:248
  26.7 1.0 %copy-start.3 = (bf16[256,1536]{1,0:T(8,128)(2,1)}, bf16[256,1536]{1,0:T(8,128)(2,1)S(1)}, u32[]{:S(2)}) copy-start(bf16[256,1536]{1,0:T(8,128)(2,1)S(1)} %shard_map.87.loc_hbm) | copy-start | bytes 2359300
  28.3 6.1 %copy-start.1 = (bf16[36,488,488]{2,1,0:T(8,128)(2,1)S(1)}, bf16[36,488,488]{2,1,0:T(8,128)(2,1)}, u32[]{:S(2)}) copy-start(bf16[36,488,488]{2,1,0:T(8,128)(2,1)} %t_ref) | copy-start | bytes 51439108
  40.8 6.5 %copy-start = (bf16[36,512,512]{2,1,0:T(8,128)(2,1)}, bf16[36,512,512]{2,1,0:T(8,128)(2,1)S(1)}, u32[]{:S(2)}) copy-start(bf16[36,512,512]{2,1,0:T(8,128)(2,1)S(1)} %shard_map.88.t_hbm) | copy-start | bytes 56623108
